TPU v7x, 256 devices: a whole 4x4x8 slice. The times are simulated.
256 devices in a mesh: blk: 16 (over y_hi, x, core), uly: 16 (over z, y_lo).
Axes of the slice: x: 4, y: 4 (y_hi: 2, y_lo: 2; y = y_hi * 2 + y_lo), z: 8, core: 2. Of those that a mesh axis runs over, the one named last changes fastest.
Arguments:
- queries: bfloat16 [32768, 6144], P(('blk', 'uly')), may hold values from -5.5 to 5.5
- keys: bfloat16 [32768, 6144], P(('blk', 'uly')), may hold values from -5.5 to 5.5
- values: bfloat16 [32768, 6144], P(('blk', 'uly')), may hold values from -6 to 6
- key_tiles: int32 [48, 256, 12], P('uly', 'blk'), may hold values from 0 to 255, as said below
- tile_mask: int32 [48, 256, 12], P('uly', 'blk'), may hold values from 0 to 1
Outputs:
- attended: bfloat16 [32768, 6144], P(('blk', 'uly'))
Inputs may be any that keep to these rules, and one draw needn't show every extreme that they name: Where tile_mask is 1, key_tiles[h, i, j] names a key tile within 8 tiles of query tile i; the tiles named with mask 1 for one query tile are distinct and always include tile i itself.
All inputs are finite; a program needn't handle non-finite values.
Results may differ from a plain program's by a relative error of at most 0.0046.
Values may be sent and summed in bfloat16 or wider, within the bound.
No kernel may reach another device: no remote copies, remote signals or barrier semaphores. Data moves between devices by JAX's collectives and lax.ppermute only.
A program may use at most 128 MiB of HBM per device.

v0:
```python
import math

import jax
import jax.numpy as jnp
from jax import lax
from jax.sharding import PartitionSpec as P

TILE = 128


def passed_along(x, axis, by):
    length = lax.axis_size(axis)
    pairs = [(i, i + by) for i in range(length) if 0 <= i + by < length]
    return lax.ppermute(x, axis, pairs)


def heads_major(matrix, heads_here, head_dim):
    return matrix.reshape(-1, TILE, heads_here, head_dim).transpose(2, 0, 1, 3)


def select_tiles(selector, flattened, head_dim):
    picked = jnp.einsum("hbje,hef->hbjf", selector, flattened, preferred_element_type=jnp.float32)
    shape = picked.shape
    return picked.astype(jnp.bfloat16).reshape(shape[0], shape[1], shape[2], TILE, head_dim)


def attend_group(query_block, gathered_keys, gathered_values, usable, factor):
    scores = (
        jnp.einsum(
            "hbtd,hbjsd->hbtjs", query_block, gathered_keys, preferred_element_type=jnp.float32
        )
        * factor
    )
    scores = jnp.where(usable[:, :, None, :, None], scores, -jnp.inf)
    highest = jnp.max(scores, axis=(3, 4), keepdims=True)
    weights = jnp.exp(scores - highest)
    totals = jnp.sum(weights, axis=(3, 4))
    summed = jnp.einsum(
        "hbtjs,hbjsd->hbtd",
        weights.astype(jnp.bfloat16),
        gathered_values,
        preferred_element_type=jnp.float32,
    )
    return (summed / totals[..., None]).astype(jnp.bfloat16)


def on_device(queries, keys, values, key_tiles, tile_mask):
    heads_here = key_tiles.shape[0]
    slab_tiles = key_tiles.shape[1]
    head_dim = queries.shape[1] // (heads_here * lax.axis_size("uly"))
    slab_rows = slab_tiles * TILE
    slab_index = lax.axis_index("blk")
    slab_queries, slab_keys, slab_values = (
        lax.all_to_all(queries, "uly", split_axis=1, concat_axis=0, tiled=True),
        lax.all_to_all(keys, "uly", split_axis=1, concat_axis=0, tiled=True),
        lax.all_to_all(values, "uly", split_axis=1, concat_axis=0, tiled=True),
    )
    key_value = jnp.stack((slab_keys, slab_values))
    earlier = passed_along(key_value, "blk", 1)
    further = passed_along(key_value, "blk", -1)
    first_tile = (slab_index - 1) * slab_tiles
    extended = jnp.concatenate((earlier, key_value, further), axis=1)
    key_heads = heads_major(extended[0], heads_here, head_dim)
    value_heads = heads_major(extended[1], heads_here, head_dim)
    query_heads = heads_major(slab_queries, heads_here, head_dim)
    extended_tiles = key_heads.shape[1]
    key_rows = key_heads.reshape(heads_here, extended_tiles, TILE * head_dim)
    value_rows = value_heads.reshape(heads_here, extended_tiles, TILE * head_dim)
    local_tiles = jnp.clip(key_tiles - first_tile, 0, extended_tiles - 1)
    usable_all = tile_mask > 0
    group_tiles = min(slab_tiles, 512 // TILE)
    factor = 1.0 / math.sqrt(head_dim)
    tile_numbers = jnp.arange(extended_tiles, dtype=jnp.int32)

    def one_group(offset):
        query_block = lax.dynamic_slice_in_dim(query_heads, offset, group_tiles, 1)
        tile_block = lax.dynamic_slice_in_dim(local_tiles, offset, group_tiles, 1)
        usable = lax.dynamic_slice_in_dim(usable_all, offset, group_tiles, 1)
        selector = (tile_block[..., None] == tile_numbers).astype(jnp.bfloat16)
        gathered_keys = select_tiles(selector, key_rows, head_dim)
        gathered_values = select_tiles(selector, value_rows, head_dim)
        return attend_group(query_block, gathered_keys, gathered_values, usable, factor)

    results = lax.map(
        one_group, jnp.arange(slab_tiles // group_tiles, dtype=jnp.int32) * group_tiles
    )
    merged = results.transpose(0, 2, 3, 1, 4).reshape(slab_rows, heads_here * head_dim)
    return lax.all_to_all(merged, "uly", split_axis=0, concat_axis=1, tiled=True)


def solution(mesh):
    placed = (
        P(("blk", "uly"), None),
        P(("blk", "uly"), None),
        P(("blk", "uly"), None),
        P("uly", "blk", None),
        P("uly", "blk", None),
    )
    return jax.shard_map(
        on_device, mesh=mesh, in_specs=placed, out_specs=P(("blk", "uly"), None), check_vma=False
    )
```

profile of v0, /device:TPU:7, one launch (start us, length us, event | category | flops | bytes accessed | tf_op | source)
XLA Modules:
  0.0 425.5 jit_solution(14068234164363223436)
XLA Ops:
  2.7 9.3 %all-to-all-start.2 = ((bf16[128,16,384]{0,2,1:T(8,128)(2,1)}), bf16[128,16,384]{0,2,1:T(8,128)(2,1)S(1)}, u32[]{:S(2)}, u32[]{:S(2)}) async-start(bf16[128,16,384]{0,2,1:T(8,128)(2,1)} %bitcast.7), calls=%async_computation.2 | async-start | bytes 3145728 | tf_op jit(solution)/shard_map/all_to_all | solution.py:56
  13.6 34.3 %all-to-all-done.2 = bf16[128,16,384]{0,2,1:T(8,128)(2,1)S(1)} async-done(((bf16[128,16,384]{0,2,1:T(8,128)(2,1)}), bf16[128,16,384]{0,2,1:T(8,128)(2,1)S(1)}, u32[]{:S(2)}, u32[]{:S(2)}) %all-to-all-start.2) | async-done | bytes 1572896 | tf_op jit(solution)/shard_map/all_to_all | solution.py:56
  47.8 7.1 %all-to-all-start.1 = ((bf16[128,16,384]{0,2,1:T(8,128)(2,1)}), bf16[128,16,384]{0,2,1:T(8,128)(2,1)}, u32[]{:S(2)}, u32[]{:S(2)}) async-start(bf16[128,16,384]{0,2,1:T(8,128)(2,1)} %bitcast.4), calls=%async_computation.1 | async-start | bytes 3145728 | tf_op jit(solution)/shard_map/all_to_all | solution.py:55
  55.8 34.7 %all-to-all-done.1 = bf16[128,16,384]{0,2,1:T(8,128)(2,1)} async-done(((bf16[128,16,384]{0,2,1:T(8,128)(2,1)}), bf16[128,16,384]{0,2,1:T(8,128)(2,1)}, u32[]{:S(2)}, u32[]{:S(2)}) %all-to-all-start.1) | async-done | bytes 1572896 | tf_op jit(solution)/shard_map/all_to_all | solution.py:55
  114.0 31.2 %collective-permute-done.1 = bf16[2,2048,384]{2,1,0:T(8,128)(2,1)} collective-permute-done((bf16[2,2048,384]{2,1,0:T(8,128)(2,1)}, bf16[2,2048,384]{2,1,0:T(8,128)(2,1)}, u32[]{:S(2)}, u32[]{:S(2)}) %collective-permute-start.1) | collective-permute-done | bytes 3145760 | tf_op jit(solution)/shard_map/ppermute | solution.py:14
  151.3 7.8 %pad_maximum_fusion = bf16[2,6144,384]{2,1,0:T(8,128)(2,1)S(1)} fusion(bf16[2,2048,384]{2,1,0:T(8,128)(2,1)} %collective-permute-done.1, bf16[1,2048,384]{2,1,0:T(8,128)(2,1)} %bitcast.92, bf16[1,2048,384]{2,1,0:T(8,128)(2,1)} %bitcast.94, bf16[2,2048,384]{2,1,0:T(8,128)(2,1)} %collective-permute-done), kind=kLoop, calls=%fused_computation.30 | loop fusion | flops 37748736 | bytes 18874368 | tf_op jit(solution)/shard_map/concatenate | solution.py:62
  176.2 7.1 %copy.29 = bf16[3,48,128,128]{3,2,1,0:T(8,128)(2,1)} copy(bf16[3,48,128,128]{2,1,3,0:T(8,128)(2,1)} %bitcast.88) | data formatting | bytes 9437184 | tf_op jit(solution)/shard_map/transpose | solution.py:18
  183.3 8.2 %reshape.38 = bf16[3,48,16384]{2,1,0:T(8,128)(2,1)} reshape(bf16[3,48,128,128]{3,2,1,0:T(8,128)(2,1)} %copy.29) | data formatting | bytes 9437184 | tf_op jit(solution)/shard_map/reshape | solution.py:67
  203.8 7.1 %copy.31 = bf16[3,48,128,128]{3,2,1,0:T(8,128)(2,1)} copy(bf16[3,48,128,128]{2,1,3,0:T(8,128)(2,1)} %bitcast.90) | data formatting | bytes 9437184 | tf_op jit(solution)/shard_map/transpose | solution.py:18
  210.9 8.3 %reshape.39 = bf16[3,48,16384]{2,1,0:T(8,128)(2,1)} reshape(bf16[3,48,128,128]{3,2,1,0:T(8,128)(2,1)} %copy.31) | data formatting | bytes 9437184 | tf_op jit(solution)/shard_map/reshape | solution.py:68
  219.2 171.5 %while.11 = (s32[]{:T(128)}, bf16[4,3,4,128,128]{3,4,1,2,0:T(8,128)(2,1)S(1)}, s32[4]{0:T(128)S(1)}, pred[3,16,12]{2,1,0:T(8,128)(4,1)S(1)}, bf16[3,16,128,128]{...) while((s32[]{:T(128)}, ...), condition=%wide.region_3.4_spmd.clone, body=%wide.region_0.3_spmd.clone.sunk | while | flops 1692019200 | bytes 93619376 | solution.py:84
  221.8 6.8 %convolution_convert_fusion.4 = bf16[3,4,12,16384]{3,2,1,0:T(8,128)(2,1)} fusion(bf16[3,48,16384]{2,1,0:T(8,128)(2,1)} %get-tuple-element.189, s32[3,4,12]{2,1,0:T(4,128)S(1)} %constant_dynamic-slice_fusion.6), kind=kOutput, calls=%fused_computation.1.clone.1 | convolution fusion | flops 228858624 | bytes 9437760 | tf_op jit(solution)/shard_map/while/body/eval_jaxpr/hbje,hef->hbjf/dot_general | solution.py:22
  228.6 7.9 %reshape.50 = bf16[3,4,12,128,128]{4,3,2,1,0:T(8,128)(2,1)} reshape(bf16[3,4,12,16384]{3,2,1,0:T(8,128)(2,1)} %convolution_convert_fusion.4) | data formatting | bytes 9437184 | tf_op jit(solution)/shard_map/while/body/eval_jaxpr/reshape | solution.py:24
  236.5 6.8 %convolution_convert_fusion.5 = bf16[3,4,12,16384]{3,2,1,0:T(8,128)(2,1)} fusion(bf16[3,48,16384]{2,1,0:T(8,128)(2,1)} %get-tuple-element.188, s32[3,4,12]{2,1,0:T(4,128)S(1)} %constant_dynamic-slice_fusion.6), kind=kOutput, calls=%fused_computation.2.clone.1 | convolution fusion | flops 228858624 | bytes 9437760 | tf_op jit(solution)/shard_map/while/body/eval_jaxpr/hbje,hef->hbjf/dot_general | solution.py:22
  243.3 7.9 %reshape.51 = bf16[3,4,12,128,128]{4,3,2,1,0:T(8,128)(2,1)} reshape(bf16[3,4,12,16384]{3,2,1,0:T(8,128)(2,1)} %convolution_convert_fusion.5) | data formatting | bytes 9437184 | tf_op jit(solution)/shard_map/while/body/eval_jaxpr/reshape | solution.py:24
  264.7 6.8 %convolution_convert_fusion.4 = bf16[3,4,12,16384]{3,2,1,0:T(8,128)(2,1)} fusion(bf16[3,48,16384]{2,1,0:T(8,128)(2,1)} %get-tuple-element.189, s32[3,4,12]{2,1,0:T(4,128)S(1)} %constant_dynamic-slice_fusion.6), kind=kOutput, calls=%fused_computation.1.clone.1 | convolution fusion | flops 228858624 | bytes 9437760 | tf_op jit(solution)/shard_map/while/body/eval_jaxpr/hbje,hef->hbjf/dot_general | solution.py:22
  271.5 7.9 %reshape.50 = bf16[3,4,12,128,128]{4,3,2,1,0:T(8,128)(2,1)} reshape(bf16[3,4,12,16384]{3,2,1,0:T(8,128)(2,1)} %convolution_convert_fusion.4) | data formatting | bytes 9437184 | tf_op jit(solution)/shard_map/while/body/eval_jaxpr/reshape | solution.py:24
  279.4 6.8 %convolution_convert_fusion.5 = bf16[3,4,12,16384]{3,2,1,0:T(8,128)(2,1)} fusion(bf16[3,48,16384]{2,1,0:T(8,128)(2,1)} %get-tuple-element.188, s32[3,4,12]{2,1,0:T(4,128)S(1)} %constant_dynamic-slice_fusion.6), kind=kOutput, calls=%fused_computation.2.clone.1 | convolution fusion | flops 228858624 | bytes 9437760 | tf_op jit(solution)/shard_map/while/body/eval_jaxpr/hbje,hef->hbjf/dot_general | solution.py:22
  286.2 7.9 %reshape.51 = bf16[3,4,12,128,128]{4,3,2,1,0:T(8,128)(2,1)} reshape(bf16[3,4,12,16384]{3,2,1,0:T(8,128)(2,1)} %convolution_convert_fusion.5) | data formatting | bytes 9437184 | tf_op jit(solution)/shard_map/while/body/eval_jaxpr/reshape | solution.py:24
  314.4 7.9 %reshape.50 = bf16[3,4,12,128,128]{4,3,2,1,0:T(8,128)(2,1)} reshape(bf16[3,4,12,16384]{3,2,1,0:T(8,128)(2,1)} %convolution_convert_fusion.4) | data formatting | bytes 9437184 | tf_op jit(solution)/shard_map/while/body/eval_jaxpr/reshape | solution.py:24
  329.1 7.9 %reshape.51 = bf16[3,4,12,128,128]{4,3,2,1,0:T(8,128)(2,1)} reshape(bf16[3,4,12,16384]{3,2,1,0:T(8,128)(2,1)} %convolution_convert_fusion.5) | data formatting | bytes 9437184 | tf_op jit(solution)/shard_map/while/body/eval_jaxpr/reshape | solution.py:24
  357.3 7.9 %reshape.50 = bf16[3,4,12,128,128]{4,3,2,1,0:T(8,128)(2,1)} reshape(bf16[3,4,12,16384]{3,2,1,0:T(8,128)(2,1)} %convolution_convert_fusion.4) | data formatting | bytes 9437184 | tf_op jit(solution)/shard_map/while/body/eval_jaxpr/reshape | solution.py:24
  372.0 7.9 %reshape.51 = bf16[3,4,12,128,128]{4,3,2,1,0:T(8,128)(2,1)} reshape(bf16[3,4,12,16384]{3,2,1,0:T(8,128)(2,1)} %convolution_convert_fusion.5) | data formatting | bytes 9437184 | tf_op jit(solution)/shard_map/while/body/eval_jaxpr/reshape | solution.py:24
  390.8 33.2 %all_to_all.67 = bf16[16,128,384]{1,2,0:T(8,128)(2,1)S(1)} all-to-all(bf16[16,128,384]{1,2,0:T(8,128)(2,1)S(1)} %bitcast.97), channel_id=1, replica_groups=mesh['blk'=16,'uly'=16] {'uly'}, dimensions={0} | all-to-all | bytes 3145728 | tf_op jit(solution)/shard_map/all_to_all | solution.py:88
  (97 shorter events, 138.6 us)
Async XLA Ops:
  0.0 12.0 %copy-start.2 = (bf16[128,6144]{1,0:T(8,128)(2,1)S(1)}, bf16[128,6144]{1,0:T(8,128)(2,1)}, u32[]{:S(2)}) copy-start(bf16[128,6144]{1,0:T(8,128)(2,1)} %param.8) | copy-start | bytes 4718596
  2.7 45.2 %all-to-all-start.2 = ((bf16[128,16,384]{0,2,1:T(8,128)(2,1)}), bf16[128,16,384]{0,2,1:T(8,128)(2,1)S(1)}, u32[]{:S(2)}, u32[]{:S(2)}) async-start(bf16[128,16,384]{0,2,1:T(8,128)(2,1)} %bitcast.7), calls=%async_computation.2 | async-start | bytes 3145728 | tf_op jit(solution)/shard_map/all_to_all | solution.py:56
  47.8 42.7 %all-to-all-start.1 = ((bf16[128,16,384]{0,2,1:T(8,128)(2,1)}), bf16[128,16,384]{0,2,1:T(8,128)(2,1)}, u32[]{:S(2)}, u32[]{:S(2)}) async-start(bf16[128,16,384]{0,2,1:T(8,128)(2,1)} %bitcast.4), calls=%async_computation.1 | async-start | bytes 3145728 | tf_op jit(solution)/shard_map/all_to_all | solution.py:55
  55.8 38.8 %copy-start = (bf16[16,128,384]{2,1,0:T(8,128)(2,1)}, bf16[16,128,384]{2,1,0:T(8,128)(2,1)S(1)}, u32[]{:S(2)}) copy-start(bf16[16,128,384]{2,1,0:T(8,128)(2,1)S(1)} %copy.27) | copy-start | bytes 4718596
  92.4 15.8 %copy-start.1 = (bf16[16,128,384]{2,1,0:T(8,128)(2,1)}, bf16[16,128,384]{2,1,0:T(8,128)(2,1)S(1)}, u32[]{:S(2)}) copy-start(bf16[16,128,384]{2,1,0:T(8,128)(2,1)S(1)} %copy.25) | copy-start | bytes 4718596
  94.6 19.3 %copy-start.5 = (s32[3,16,12]{2,1,0:T(8,128)S(1)}, s32[3,16,12]{2,1,0:T(8,128)}, u32[]{:S(2)}) copy-start(s32[3,16,12]{2,1,0:T(8,128)} %param.11) | copy-start | bytes 6916
  94.6 19.4 %copy-start.4 = (s32[3,16,12]{2,1,0:T(8,128)S(1)}, s32[3,16,12]{2,1,0:T(8,128)}, u32[]{:S(2)}) copy-start(s32[3,16,12]{2,1,0:T(8,128)} %param.10) | copy-start | bytes 6916
  94.6 50.5 %collective-permute-start.1 = (bf16[2,2048,384]{2,1,0:T(8,128)(2,1)}, bf16[2,2048,384]{2,1,0:T(8,128)(2,1)}, u32[]{:S(2)}, u32[]{:S(2)}) collective-permute-start(bf16[2,2048,384]{2,1,0:T(8,128)(2,1)} %pad_maximum_fusion.1), channel_id=1, source_target_pairs={{16,0},{32,16},{48,32},{64,48},{80,64},{96,80},{112,96},{128,112},... | collective-permute-start | bytes 9437192 | tf_op jit(solution)/shard_map/ppermute | solution.py:14
  101.3 50.0 %collective-permute-start = (bf16[2,2048,384]{2,1,0:T(8,128)(2,1)}, bf16[2,2048,384]{2,1,0:T(8,128)(2,1)}, u32[]{:S(2)}, u32[]{:S(2)}) collective-permute-start(bf16[2,2048,384]{2,1,0:T(8,128)(2,1)} %pad_maximum_fusion.1), channel_id=1, source_target_pairs={{0,16},{16,32},{32,48},{48,64},{64,80},{80,96},{96,112},{112,128},... | collective-permute-start | bytes 9437192 | tf_op jit(solution)/shard_map/ppermute | solution.py:14
  108.2 111.0 %all-to-all-start = ((bf16[128,16,384]{0,2,1:T(8,128)(2,1)}), bf16[128,16,384]{0,2,1:T(8,128)(2,1)}, u32[]{:S(2)}, u32[]{:S(2)}) async-start(bf16[128,16,384]{0,2,1:T(8,128)(2,1)} %bitcast), calls=%async_computation | async-start | bytes 3145728 | tf_op jit(solution)/shard_map/all_to_all | solution.py:54
  210.9 8.3 %copy-start.3 = (bf16[4,3,4,128,128]{3,4,1,2,0:T(8,128)(2,1)S(1)}, bf16[4,3,4,128,128]{3,4,1,2,0:T(8,128)(2,1)}, u32[]{:S(2)}) copy-start(bf16[4,3,4,128,128]{3,4,1,2,0:T(8,128)(2,1)} %custom-call) | copy-start | bytes 4718596
  252.3 6.0 %slice-start = ((s8[4718592]{0:T(1024)(128)(4,1)}), s8[524288]{0:T(1024)(128)(4,1)S(1)}, s32[]{:S(2)}) async-start(s8[4718592]{0:T(1024)(128)(4,1)} %bitcast.85), calls=%async_computation.4 | async-start | bytes 1048576 | tf_op jit(solution)/shard_map/while
  252.5 5.8 %slice-start.1 = ((s8[4718592]{0:T(1024)(128)(4,1)}), s8[4194304]{0:T(1024)(128)(4,1)S(1)}, s32[]{:S(2)}) async-start(s8[4718592]{0:T(1024)(128)(4,1)} %bitcast.85), calls=%async_computation.5 | async-start | bytes 8388608 | tf_op jit(solution)/shard_map/while
  295.2 6.0 %slice-start = ((s8[4718592]{0:T(1024)(128)(4,1)}), s8[524288]{0:T(1024)(128)(4,1)S(1)}, s32[]{:S(2)}) async-start(s8[4718592]{0:T(1024)(128)(4,1)} %bitcast.85), calls=%async_computation.4 | async-start | bytes 1048576 | tf_op jit(solution)/shard_map/while
  295.4 5.8 %slice-start.1 = ((s8[4718592]{0:T(1024)(128)(4,1)}), s8[4194304]{0:T(1024)(128)(4,1)S(1)}, s32[]{:S(2)}) async-start(s8[4718592]{0:T(1024)(128)(4,1)} %bitcast.85), calls=%async_computation.5 | async-start | bytes 8388608 | tf_op jit(solution)/shard_map/while
  338.1 6.0 %slice-start = ((s8[4718592]{0:T(1024)(128)(4,1)}), s8[524288]{0:T(1024)(128)(4,1)S(1)}, s32[]{:S(2)}) async-start(s8[4718592]{0:T(1024)(128)(4,1)} %bitcast.85), calls=%async_computation.4 | async-start | bytes 1048576 | tf_op jit(solution)/shard_map/while
  338.3 5.8 %slice-start.1 = ((s8[4718592]{0:T(1024)(128)(4,1)}), s8[4194304]{0:T(1024)(128)(4,1)S(1)}, s32[]{:S(2)}) async-start(s8[4718592]{0:T(1024)(128)(4,1)} %bitcast.85), calls=%async_computation.5 | async-start | bytes 8388608 | tf_op jit(solution)/shard_map/while
  380.9 6.0 %slice-start = ((s8[4718592]{0:T(1024)(128)(4,1)}), s8[524288]{0:T(1024)(128)(4,1)S(1)}, s32[]{:S(2)}) async-start(s8[4718592]{0:T(1024)(128)(4,1)} %bitcast.85), calls=%async_computation.4 | async-start | bytes 1048576 | tf_op jit(solution)/shard_map/while
  381.2 5.8 %slice-start.1 = ((s8[4718592]{0:T(1024)(128)(4,1)}), s8[4194304]{0:T(1024)(128)(4,1)S(1)}, s32[]{:S(2)}) async-start(s8[4718592]{0:T(1024)(128)(4,1)} %bitcast.85), calls=%async_computation.5 | async-start | bytes 8388608 | tf_op jit(solution)/shard_map/while
where the time goes:
time: 433 us; the launch traced here: 426 us
  local copies, waits for them, and re-layouts  143 us (33%)
  waiting for transfers between devices  106 us (24%)
  matrix products  82.4 us (19%)
  blocking collectives  33.2 us (8%)
  starting transfers between devices  33.1 us (8%)
  other arithmetic  19.2 us (4%)
  loops' own time  8.19 us (2%)
    reshape x8, local copies, waits for them, and re-layouts, select_tiles(): picked.astype(jnp.bfloat16)  63.1 us
    dot_general x8, matrix products, select_tiles(): jnp.einsum('hbje,hef->hbjf', selector, flattened, preferred_element_type=...  54.6 us
    ppermute x2, waiting for transfers between devices, passed_along(): return lax.ppermute(x, axis, pairs)  37.3 us
    all_to_all x1, waiting for transfers between devices, on_device(): lax.all_to_all(keys, 'uly', split_axis=1, concat_axis=0, tiled=True)  34.7 us
    all_to_all x1, waiting for transfers between devices, on_device(): lax.all_to_all(values, 'uly', split_axis=1, concat_axis=0, tiled=True)  34.3 us
    all_to_all x1, blocking collectives, on_device(): lax.all_to_all(merged, 'uly', split_axis=0, concat_axis=1, tiled=True)  33.2 us
    unnamed x17, local copies, waits for them, and re-layouts  18.4 us
    transpose x2, local copies, waits for them, and re-layouts, heads_major(): return matrix.reshape(-1, TILE, heads_here, head_dim).transpose(2, 0, 1, 3)  14.2 us
  transfers between devices with their start and end apart: 5, of which 4 were waited for; matrix products, arithmetic and copies ran while one was open for 17% of the time, Pallas kernels for 0%

commit v1 on v0

v1 whole, which is shorter than its diff:
```python
import functools
import math

import jax
import jax.numpy as jnp
from jax import lax
from jax.experimental import pallas as pl
from jax.experimental.pallas import tpu as pltpu
from jax.sharding import PartitionSpec as P

TILE = 128
HEAD_DIM = 128
REACH = 8
HEAD_SETS = (2, 1)
VMEM_LIMIT = 48 * 1024 * 1024


def passed_along(x, axis, by):
    length = lax.axis_size(axis)
    pairs = [(i, i + by) for i in range(length) if 0 <= i + by < length]
    return lax.ppermute(x, axis, pairs)


def exchanged(x):
    return lax.all_to_all(x, "uly", split_axis=0, concat_axis=0, tiled=True)


def pack_kernel(widths, *refs):
    inputs, outputs = refs[:3], refs[3:]
    for which, ref in enumerate(inputs):
        per_group = sum(widths)
        for group in range(ref.shape[1] // per_group):
            column = group * per_group
            for out, width in zip(outputs, widths):
                out[group, which] = ref[:, column : column + width]
                column += width


def pack(queries, keys, values, groups, widths):
    per_step = 4
    columns = per_step * sum(widths)
    return pl.pallas_call(
        functools.partial(pack_kernel, widths),
        grid=(groups // per_step,),
        in_specs=[pl.BlockSpec((TILE, columns), lambda g: (0, g))] * 3,
        out_specs=[
            pl.BlockSpec((per_step, 3, TILE, width), lambda g: (g, 0, 0, 0)) for width in widths
        ],
        out_shape=[
            jax.ShapeDtypeStruct((groups, 3, TILE, width), jnp.bfloat16) for width in widths
        ],
        compiler_params=pltpu.CompilerParams(vmem_limit_bytes=VMEM_LIMIT),
        name="pack",
    )(queries, keys, values)


def unpack_kernel(widths, *refs):
    inputs, out = refs[:-1], refs[-1]
    per_group = sum(widths)
    for group in range(out.shape[1] // per_group):
        column = group * per_group
        for ref, width in zip(inputs, widths):
            out[:, column : column + width] = ref[group]
            column += width


def unpack(parts, groups, widths):
    per_step = 4
    columns = per_step * sum(widths)
    return pl.pallas_call(
        functools.partial(unpack_kernel, widths),
        grid=(groups // per_step,),
        in_specs=[
            pl.BlockSpec((per_step, TILE, width), lambda g: (g, 0, 0)) for width in widths
        ],
        out_specs=pl.BlockSpec((TILE, columns), lambda g: (0, g)),
        out_shape=jax.ShapeDtypeStruct((TILE, groups * sum(widths)), jnp.bfloat16),
        compiler_params=pltpu.CompilerParams(vmem_limit_bytes=VMEM_LIMIT),
        name="unpack",
    )(*parts)


def attend_kernel(
    heads, slots, tile_ref, mask_ref, own, earlier, further, out, query, window, sems
):
    slab_tiles = own.shape[0]
    reach = earlier.shape[0]
    copies = [
        pltpu.make_async_copy(own.at[:, 0], query, sems.at[0]),
        pltpu.make_async_copy(
            own.at[:, pl.ds(1, 2)], window.at[pl.ds(reach, slab_tiles)], sems.at[1]
        ),
        pltpu.make_async_copy(earlier, window.at[pl.ds(0, reach)], sems.at[2]),
        pltpu.make_async_copy(further, window.at[pl.ds(reach + slab_tiles, reach)], sems.at[3]),
    ]
    for copy in copies:
        copy.start()
    for copy in copies:
        copy.wait()
    factor = math.log2(math.e) / math.sqrt(HEAD_DIM)

    def one_tile(i, carry):
        for head in range(heads):
            lanes = pl.ds(head * HEAD_DIM, HEAD_DIM)
            first = (head * slab_tiles + i) * slots
            indices = [tile_ref[first + j] for j in range(slots)]
            shut = [
                jnp.where(mask_ref[first + j] > 0, 0.0, -jnp.inf).astype(jnp.float32)
                for j in range(slots)
            ]
            tile_queries = query[i, :, lanes]
            scores = []
            for j in range(slots):
                product = lax.dot_general(
                    tile_queries,
                    window[indices[j], 0, :, lanes],
                    (((1,), (1,)), ((), ())),
                    preferred_element_type=jnp.float32,
                )
                scores.append(product * factor + shut[j])
            highest = jnp.max(functools.reduce(jnp.maximum, scores), axis=1, keepdims=True)
            weights = [jnp.exp2(score - highest) for score in scores]
            totals = jnp.sum(functools.reduce(jnp.add, weights), axis=1, keepdims=True)
            summed = jnp.dot(
                jnp.concatenate([weight.astype(jnp.bfloat16) for weight in weights], axis=1),
                jnp.concatenate([window[index, 1, :, lanes] for index in indices], axis=0),
                preferred_element_type=jnp.float32,
            )
            out[i, :, lanes] = (summed / totals).astype(jnp.bfloat16)
        return carry

    lax.fori_loop(0, slab_tiles, one_tile, 0)


def attend(tiles, mask, own, earlier, further):
    heads, slab_tiles, slots = tiles.shape
    width = own.shape[-1]
    reach = earlier.shape[0]
    window_tiles = slab_tiles + 2 * reach
    pairs = heads * slab_tiles * slots
    return pl.pallas_call(
        functools.partial(attend_kernel, heads, slots),
        in_specs=[pl.BlockSpec(memory_space=pltpu.SMEM)] * 2
        + [pl.BlockSpec(memory_space=pl.ANY)] * 3,
        out_specs=pl.BlockSpec(memory_space=pltpu.VMEM),
        out_shape=jax.ShapeDtypeStruct((slab_tiles, TILE, width), jnp.bfloat16),
        scratch_shapes=[
            pltpu.VMEM((slab_tiles, TILE, width), jnp.bfloat16),
            pltpu.VMEM((window_tiles, 2, TILE, width), jnp.bfloat16),
            pltpu.SemaphoreType.DMA((4,)),
        ],
        compiler_params=pltpu.CompilerParams(vmem_limit_bytes=VMEM_LIMIT),
        cost_estimate=pl.CostEstimate(
            flops=4 * pairs * TILE * TILE * HEAD_DIM,
            bytes_accessed=2 * TILE * width * (2 * slab_tiles + 2 * window_tiles),
            transcendentals=pairs * TILE * TILE,
        ),
        name="attend",
    )(tiles.reshape(-1), mask.reshape(-1), own, earlier, further)


def on_device(queries, keys, values, key_tiles, tile_mask):
    slab_tiles = key_tiles.shape[1]
    groups = lax.axis_size("uly")
    first_tile = lax.axis_index("blk") * slab_tiles - REACH
    local_tiles = jnp.clip(key_tiles - first_tile, 0, slab_tiles + 2 * REACH - 1)
    widths = [heads * HEAD_DIM for heads in HEAD_SETS]
    packed = pack(queries, keys, values, groups, widths)
    received = []
    for part in packed:
        if received:
            part, received[-1] = lax.optimization_barrier((part, received[-1]))
        received.append(exchanged(part))
    results = []
    head = 0
    for heads, own in zip(HEAD_SETS, received):
        earlier = passed_along(own[slab_tiles - REACH :, 1:], "blk", 1)
        further = passed_along(own[:REACH, 1:], "blk", -1)
        attended = attend(
            local_tiles[head : head + heads],
            tile_mask[head : head + heads],
            own,
            earlier,
            further,
        )
        head += heads
        results.append(exchanged(attended))
    return unpack(results, groups, widths)


def solution(mesh):
    placed = (
        P(("blk", "uly"), None),
        P(("blk", "uly"), None),
        P(("blk", "uly"), None),
        P("uly", "blk", None),
        P("uly", "blk", None),
    )
    return jax.shard_map(
        on_device, mesh=mesh, in_specs=placed, out_specs=P(("blk", "uly"), None), check_vma=False
    )
```

time: 433 us -> 222 us (0.51); the launches traced: 426 us -> 221 us
  local copies, waits for them, and re-layouts: 143 us -> 10.3 us
  matrix products: 82.4 us -> 0 us
  waiting for transfers between devices: 106 us -> 34.2 us
  blocking collectives: 33.2 us -> 102 us
  Pallas kernels: 0 us -> 44.2 us
  other arithmetic: 19.2 us -> 0.01 us
  loops' own time: 8.19 us -> 0 us
    dot_general x16 -> x0, matrix products: 82.4 us -> none  [the longest x8 54.6 us: select_tiles(): jnp.einsum('hbje,hef->hbjf', selector, flattened, preferred_element_type=...]
    reshape x10 -> x4, local copies, waits for them, and re-layouts: 79.6 us -> 0.37 us  [the longest x2 0.19 us: attend(): tiles.reshape(-1)]
    all_to_all x3 -> x2, waiting for transfers between devices: 69 us -> 0.01 us  [exchanged(): return lax.all_to_all(x, 'uly', split_axis=0, concat_axis=0, tiled=True)]
    all_to_all x1 -> x2, blocking collectives: 33.2 us -> 102 us  [exchanged(): return lax.all_to_all(x, 'uly', split_axis=0, concat_axis=0, tiled=True)]
    pallas_call x0 -> x4, Pallas kernels: none -> 44.2 us  [the longest x2 38.1 us: attend(): pl.pallas_call(functools.partial(attend_kernel, heads, slots), in_specs=[...]
    transpose x2 -> x0, local copies, waits for them, and re-layouts: 14.2 us -> none  [heads_major(): return matrix.reshape(-1, TILE, heads_here, head_dim).transpose(2, 0, 1, 3)]
    slice x3 -> x8, local copies, waits for them, and re-layouts: 17.9 us -> 4.25 us  [the longest x2 4.23 us: on_device(): further = passed_along(own[:REACH, 1:], 'blk', -1)]
    unnamed x17 -> x12, local copies, waits for them, and re-layouts: 18.4 us -> 5.67 us
  transfers between devices with their start and end apart: 5 -> 6, of which waited for: 4 -> 4; matrix products, arithmetic and copies ran while one was open for 17% -> 2% of each run, Pallas kernels for 0% -> 17%
where the time goes in v1:
time: 222 us; the launch traced here: 221 us
  blocking collectives  102 us (46%)
  Pallas kernels  44.2 us (20%)
  waiting for transfers between devices  34.2 us (15%)
  starting transfers between devices  30.7 us (14%)
  local copies, waits for them, and re-layouts  10.3 us (5%)
    all_to_all x2, blocking collectives, exchanged(): return lax.all_to_all(x, 'uly', split_axis=0, concat_axis=0, tiled=True)  102 us
    pallas_call x2, Pallas kernels, attend(): pl.pallas_call(functools.partial(attend_kernel, heads, slots), in_specs=[...  38.1 us
    ppermute x4, waiting for transfers between devices, passed_along(): return lax.ppermute(x, axis, pairs)  34.2 us
    all_to_all x2, starting transfers between devices, exchanged(): return lax.all_to_all(x, 'uly', split_axis=0, concat_axis=0, tiled=True)  18.7 us
    ppermute x4, starting transfers between devices, passed_along(): return lax.ppermute(x, axis, pairs)  12 us
    unnamed x12, local copies, waits for them, and re-layouts  5.67 us
  transfers between devices with their start and end apart: 6, of which 4 were waited for; matrix products, arithmetic and copies ran while one was open for 2% of the time, Pallas kernels for 17%

profile of v1, /device:TPU:7, one launch (start us, length us, event | category | flops | bytes accessed | tf_op | source)
XLA Modules:
  0.0 221.3 jit_solution(3278127001052319721)
XLA Ops:
  0.0 1.4 copy-done
  1.4 1.4 copy-done.1
  2.8 4.4 %pack.1 = (bf16[16,3,128,256]{3,2,1,0:T(8,128)(2,1)}, bf16[16,3,128,128]{3,2,1,0:T(8,128)(2,1)}) custom-call(bf16[128,6144]{1,0:T(8,128)(2,1)S(1)} %copy-done, bf16[128,6144]{1,0:T(8,128)(2,1)S(1)} %copy-done.1, bf16[128,6144]{1,0:T(8,128)(2,1)} %refs_2_.1), custom_call_target="tpu_custom_call" | custom-call | tf_op jit(solution)/shard_map/pack/pallas_call | solution.py:42
  7.2 81.2 %all_to_all.20.own = bf16[16,3,128,256]{3,2,1,0:T(8,128)(2,1)} all-to-all(bf16[16,3,128,256]{3,2,1,0:T(8,128)(2,1)} %get-tuple-element.10), channel_id=1, replica_groups=mesh['blk'=16,'uly'=16] {'uly'}, dimensions={0} | all-to-all | bytes 6291456 | tf_op jit(solution)/shard_map/all_to_all | solution.py:25
  88.4 4.8 %all-to-all-start.2 = ((bf16[16,3,128,128]{3,2,1,0:T(8,128)(2,1)}), bf16[16,3,128,128]{3,2,1,0:T(8,128)(2,1)S(1)}, u32[]{:S(2)}, u32[]{:S(2)}) async-start(bf16[16,3,128,128]{3,2,1,0:T(8,128)(2,1)} %get-tuple-element.12), calls=%async_computation.2 | async-start | bytes 3145728 | tf_op jit(solution)/shard_map/all_to_all | solution.py:25
  93.2 3.1 %fusion = (bf16[8,2,128,256]{3,2,1,0:T(8,128)(2,1)}, bf16[8,2,128,256]{3,2,1,0:T(8,128)(2,1)}) fusion(bf16[16,3,128,256]{3,2,1,0:T(8,128)(2,1)} %all_to_all.20.own), kind=kLoop, calls=%fused_computation.1 | loop fusion | bytes 4194304 | tf_op jit(solution)/shard_map/slice | solution.py:178
  96.3 5.7 %collective-permute-start = (bf16[8,2,128,256]{3,2,1,0:T(8,128)(2,1)}, bf16[8,2,128,256]{3,2,1,0:T(8,128)(2,1)S(1)}, u32[]{:S(2)}, u32[]{:S(2)}) collective-permute-start(bf16[8,2,128,256]{3,2,1,0:T(8,128)(2,1)} %get-tuple-element.14), channel_id=1, source_target_pairs={{0,16},{16,32},{32,48},{48,64},{64,80},{80,96},{96,112},{112,128},... | collective-permute-start | bytes 3145736 | tf_op jit(solution)/shard_map/ppermute | solution.py:21
  102.1 1.9 collective-permute-start.1
  104.0 0.1 reshape.12.tile_ref
  104.3 12.6 %collective-permute-done.earlier = bf16[8,2,128,256]{3,2,1,0:T(8,128)(2,1)S(1)} collective-permute-done((bf16[8,2,128,256]{3,2,1,0:T(8,128)(2,1)}, bf16[8,2,128,256]{3,2,1,0:T(8,128)(2,1)S(1)}, u32[]{:S(2)}, u32[]{:S(2)}) %collective-permute-start) | collective-permute-done | bytes 1048608 | tf_op jit(solution)/shard_map/ppermute | solution.py:21
  116.9 10.5 %collective-permute-done.1.further = bf16[8,2,128,256]{3,2,1,0:T(8,128)(2,1)} collective-permute-done((bf16[8,2,128,256]{3,2,1,0:T(8,128)(2,1)}, bf16[8,2,128,256]{3,2,1,0:T(8,128)(2,1)}, u32[]{:S(2)}, u32[]{:S(2)}) %collective-permute-start.1) | collective-permute-done | bytes 1048608 | tf_op jit(solution)/shard_map/ppermute | solution.py:21
  127.4 24.1 %attend.2 = bf16[16,128,256]{2,1,0:T(8,128)(2,1)S(1)} custom-call(s32[384]{0:T(512)S(1)} %reshape.12.tile_ref, s32[384]{0:T(512)S(1)} %reshape.13.mask_ref, bf16[16,3,128,256]{3,2,1,0:T(8,128)(2,1)} %all_to_all.20.own, bf16[8,2,128,256]{3,2,1,0:T(8,128)(2,1)S(1)} %collective-permute-done.earlier, bf16[8,2,128,256]{3,2,1,0:T(8,128)(2,1)} %collective-permute-done.1.further), custom_call_target="tpu_custom_call" | custom-call | flops 3221225472 | bytes 6291456 | tf_op jit(solution)/shard_map/attend/pallas_call | solution.py:141
  151.5 1.0 copy-done.2
  152.5 13.9 %all-to-all-start.1 = ((bf16[16,128,256]{2,1,0:T(8,128)(2,1)}), bf16[16,128,256]{2,1,0:T(8,128)(2,1)S(1)}, u32[]{:S(2)}, u32[]{:S(2)}) async-start(bf16[16,128,256]{2,1,0:T(8,128)(2,1)} %copy-done.2), calls=%async_computation.1 | async-start | bytes 2097152 | tf_op jit(solution)/shard_map/all_to_all | solution.py:25
  166.4 1.1 fusion.1
  167.5 1.9 collective-permute-start.2
  169.4 2.4 %collective-permute-start.3 = (bf16[8,2,128,128]{3,2,1,0:T(8,128)(2,1)}, bf16[8,2,128,128]{3,2,1,0:T(8,128)(2,1)}, u32[]{:S(2)}, u32[]{:S(2)}) collective-permute-start(bf16[8,2,128,128]{3,2,1,0:T(8,128)(2,1)} %get-tuple-element.15), channel_id=1, source_target_pairs={{16,0},{32,16},{48,32},{64,48},{80,64},{96,80},{112,96},{128,112},... | collective-permute-start | bytes 1572872 | tf_op jit(solution)/shard_map/ppermute | solution.py:21
  172.0 3.8 %collective-permute-done.2.earlier = bf16[8,2,128,128]{3,2,1,0:T(8,128)(2,1)S(1)} collective-permute-done((bf16[8,2,128,128]{3,2,1,0:T(8,128)(2,1)}, bf16[8,2,128,128]{3,2,1,0:T(8,128)(2,1)S(1)}, u32[]{:S(2)}, u32[]{:S(2)}) %collective-permute-start.2) | collective-permute-done | bytes 524320 | tf_op jit(solution)/shard_map/ppermute | solution.py:21
  175.8 0.8 copy-done.3
  176.7 7.3 %collective-permute-done.3.further = bf16[8,2,128,128]{3,2,1,0:T(8,128)(2,1)} collective-permute-done((bf16[8,2,128,128]{3,2,1,0:T(8,128)(2,1)}, bf16[8,2,128,128]{3,2,1,0:T(8,128)(2,1)}, u32[]{:S(2)}, u32[]{:S(2)}) %collective-permute-start.3) | collective-permute-done | bytes 524320 | tf_op jit(solution)/shard_map/ppermute | solution.py:21
  184.0 1.0 copy-done.4
  185.0 14.1 %attend.3 = bf16[16,128,128]{2,1,0:T(8,128)(2,1)S(1)} custom-call(s32[192]{0:T(256)S(1)} %reshape.14.tile_ref, s32[192]{0:T(256)S(1)} %reshape.15.mask_ref, bf16[16,3,128,128]{3,2,1,0:T(8,128)(2,1)S(1)} %all-to-all-done.2.own, bf16[8,2,128,128]{3,2,1,0:T(8,128)(2,1)S(1)} %copy-done.4, bf16[8,2,128,128]{3,2,1,0:T(8,128)(2,1)} %collective-permute-done.3.further), custom_call_target="tpu_custom_call" | custom-call | flops 1610612736 | bytes 3145728 | tf_op jit(solution)/shard_map/attend/pallas_call | solution.py:141
  199.1 20.5 %all_to_all.21.refs_1_ = bf16[16,128,128]{2,1,0:T(8,128)(2,1)S(1)} all-to-all(bf16[16,128,128]{2,1,0:T(8,128)(2,1)S(1)} %attend.3), channel_id=1, replica_groups=mesh['blk'=16,'uly'=16] {'uly'}, dimensions={0} | all-to-all | bytes 1048576 | tf_op jit(solution)/shard_map/all_to_all | solution.py:25
  219.6 1.7 unpack.1
  (19 shorter events, 0.3 us)
Async XLA Ops:
  0.0 1.4 copy-start
  1.4 1.4 copy-start.1
  88.4 64.1 %all-to-all-start.2 = ((bf16[16,3,128,128]{3,2,1,0:T(8,128)(2,1)}), bf16[16,3,128,128]{3,2,1,0:T(8,128)(2,1)S(1)}, u32[]{:S(2)}, u32[]{:S(2)}) async-start(bf16[16,3,128,128]{3,2,1,0:T(8,128)(2,1)} %get-tuple-element.12), calls=%async_computation.2 | async-start | bytes 3145728 | tf_op jit(solution)/shard_map/all_to_all | solution.py:25
  93.2 10.8 %copy-start.5 = (s32[3,16,12]{2,1,0:T(8,128)S(1)}, s32[3,16,12]{2,1,0:T(8,128)}, u32[]{:S(2)}) copy-start(s32[3,16,12]{2,1,0:T(8,128)} %param.8) | copy-start | bytes 6916
  93.2 10.9 %slice-start = ((s32[3,16,12]{2,1,0:T(8,128)}), s32[2,16,12]{2,1,0:T(8,128)S(1)}, s32[]{:S(2)}) async-start(s32[3,16,12]{2,1,0:T(8,128)} %param.9), calls=%async_computation.4 | async-start | bytes 32768 | tf_op jit(solution)/shard_map/slice | solution.py:181
  96.3 20.6 %collective-permute-start = (bf16[8,2,128,256]{3,2,1,0:T(8,128)(2,1)}, bf16[8,2,128,256]{3,2,1,0:T(8,128)(2,1)S(1)}, u32[]{:S(2)}, u32[]{:S(2)}) collective-permute-start(bf16[8,2,128,256]{3,2,1,0:T(8,128)(2,1)} %get-tuple-element.14), channel_id=1, source_target_pairs={{0,16},{16,32},{32,48},{48,64},{64,80},{80,96},{96,112},{112,128},... | collective-permute-start | bytes 3145736 | tf_op jit(solution)/shard_map/ppermute | solution.py:21
  102.1 25.3 %collective-permute-start.1 = (bf16[8,2,128,256]{3,2,1,0:T(8,128)(2,1)}, bf16[8,2,128,256]{3,2,1,0:T(8,128)(2,1)}, u32[]{:S(2)}, u32[]{:S(2)}) collective-permute-start(bf16[8,2,128,256]{3,2,1,0:T(8,128)(2,1)} %get-tuple-element.13), channel_id=1, source_target_pairs={{16,0},{32,16},{48,32},{64,48},{80,64},{96,80},{112,96},{128,112},... | collective-permute-start | bytes 3145736 | tf_op jit(solution)/shard_map/ppermute | solution.py:21
  151.5 1.0 copy-start.2
  152.5 46.6 %all-to-all-start.1 = ((bf16[16,128,256]{2,1,0:T(8,128)(2,1)}), bf16[16,128,256]{2,1,0:T(8,128)(2,1)S(1)}, u32[]{:S(2)}, u32[]{:S(2)}) async-start(bf16[16,128,256]{2,1,0:T(8,128)(2,1)} %copy-done.2), calls=%async_computation.1 | async-start | bytes 2097152 | tf_op jit(solution)/shard_map/all_to_all | solution.py:25
  166.4 5.6 %slice-start.1 = ((s32[3,16,12]{2,1,0:T(8,128)}), s32[1,16,12]{2,1,0:T(8,128)S(1)}, s32[]{:S(2)}) async-start(s32[3,16,12]{2,1,0:T(8,128)} %param.9), calls=%async_computation.5 | async-start | bytes 16384 | tf_op jit(solution)/shard_map/slice | solution.py:181
  167.5 8.3 %collective-permute-start.2 = (bf16[8,2,128,128]{3,2,1,0:T(8,128)(2,1)}, bf16[8,2,128,128]{3,2,1,0:T(8,128)(2,1)S(1)}, u32[]{:S(2)}, u32[]{:S(2)}) collective-permute-start(bf16[8,2,128,128]{3,2,1,0:T(8,128)(2,1)} %get-tuple-element.16), channel_id=1, source_target_pairs={{0,16},{16,32},{32,48},{48,64},{64,80},{80,96},{96,112},{112,128},... | collective-permute-start | bytes 1572872 | tf_op jit(solution)/shard_map/ppermute | solution.py:21
  169.4 14.5 %collective-permute-start.3 = (bf16[8,2,128,128]{3,2,1,0:T(8,128)(2,1)}, bf16[8,2,128,128]{3,2,1,0:T(8,128)(2,1)}, u32[]{:S(2)}, u32[]{:S(2)}) collective-permute-start(bf16[8,2,128,128]{3,2,1,0:T(8,128)(2,1)} %get-tuple-element.15), channel_id=1, source_target_pairs={{16,0},{32,16},{48,32},{64,48},{80,64},{96,80},{112,96},{128,112},... | collective-permute-start | bytes 1572872 | tf_op jit(solution)/shard_map/ppermute | solution.py:21
  175.8 0.8 copy-start.3
  184.0 1.0 copy-start.4

commit v2 on v1

v2 whole, which is shorter than its diff:
```python
import functools
import math

import jax
import jax.numpy as jnp
from jax import lax
from jax.experimental import pallas as pl
from jax.experimental.pallas import tpu as pltpu
from jax.sharding import PartitionSpec as P

TILE = 128
HEAD_DIM = 128
HEAD_SETS = (2, 1)
REACH = 8
PACK_VMEM = 12 * 1024 * 1024
FIRST_PACK_VMEM = 63 * 1024 * 1024
ATTEND_VMEM = 24 * 1024 * 1024


def flipped(slab, slabs):
    return slab // (slabs // 2)


def to_neighbour(x, by):
    slabs, groups = lax.axis_size("blk"), lax.axis_size("uly")
    pairs = []
    for slab in range(slabs):
        other = slab + by
        if 0 <= other < slabs:
            turn = flipped(slab, slabs) ^ flipped(other, slabs)
            for device in range(groups):
                pairs.append((slab * groups + device, other * groups + (device ^ turn)))
    return lax.ppermute(x, ("blk", "uly"), pairs)


def to_holder(x):
    slabs, groups = lax.axis_size("blk"), lax.axis_size("uly")
    pairs = [
        (slab * groups + device, slab * groups + (device ^ flipped(slab, slabs)))
        for slab in range(slabs)
        for device in range(groups)
    ]
    return lax.ppermute(x, ("blk", "uly"), pairs)


def exchanged(x):
    return lax.all_to_all(x, "uly", split_axis=0, concat_axis=0, tiled=True)


def pack_kernel(per_group, skipped, chunks, turn_ref, *refs):
    inputs, (out, held, arrived, left) = refs[:3], refs[3:]
    groups, width = out.shape[0], out.shape[-1]
    per_chunk = groups // chunks
    span = per_chunk * per_group
    taken, sent = [], []
    for chunk in range(chunks):
        for which, ref in enumerate(inputs):
            here = pl.ds(chunk * span, span)
            copy = pltpu.make_async_copy(
                ref.at[:, here], held.at[which, :, here], arrived.at[which, chunk]
            )
            copy.start()
            taken.append((chunk, which, copy))
    for chunk, which, copy in taken:
        copy.wait()
        for group in range(chunk * per_chunk, (chunk + 1) * per_chunk):
            copy = pltpu.make_async_copy(
                held.at[which, :, pl.ds(group * per_group + skipped, width)],
                out.at[group ^ turn_ref[0], which],
                left.at[which, group],
            )
            copy.start()
            sent.append(copy)
    for copy in sent:
        copy.wait()


def pack(inputs, turn, groups, skipped, width, vmem):
    chunks = 4
    rows, columns = inputs[0].shape
    return pl.pallas_call(
        functools.partial(pack_kernel, columns // groups, skipped, chunks),
        in_specs=[pl.BlockSpec(memory_space=pltpu.SMEM)]
        + [pl.BlockSpec(memory_space=pltpu.HBM)] * 3,
        out_specs=pl.BlockSpec(memory_space=pltpu.HBM),
        out_shape=jax.ShapeDtypeStruct((groups, 3, rows, width), jnp.bfloat16),
        scratch_shapes=[
            pltpu.VMEM((3, rows, columns), jnp.bfloat16),
            pltpu.SemaphoreType.DMA((3, chunks)),
            pltpu.SemaphoreType.DMA((3, groups)),
        ],
        compiler_params=pltpu.CompilerParams(vmem_limit_bytes=vmem),
        cost_estimate=pl.CostEstimate(
            flops=0, bytes_accessed=2 * 3 * rows * (columns + groups * width), transcendentals=0
        ),
        name="pack",
    )(turn, *inputs)


def unpack_kernel(widths, turn_ref, *refs):
    inputs, out = refs[:-1], refs[-1]
    per_group = sum(widths)
    for group in range(out.shape[1] // per_group):
        column = group * per_group
        for ref, width in zip(inputs, widths):
            out[:, column : column + width] = ref[group ^ turn_ref[0]]
            column += width


def unpack(parts, turn, groups):
    widths = [part.shape[-1] for part in parts]
    per_step = 4
    columns = per_step * sum(widths)
    return pl.pallas_call(
        functools.partial(unpack_kernel, widths),
        grid=(groups // per_step,),
        in_specs=[pl.BlockSpec(memory_space=pltpu.SMEM)]
        + [pl.BlockSpec((per_step, TILE, width), lambda g: (g, 0, 0)) for width in widths],
        out_specs=pl.BlockSpec((TILE, columns), lambda g: (0, g)),
        out_shape=jax.ShapeDtypeStruct((TILE, groups * sum(widths)), jnp.bfloat16),
        compiler_params=pltpu.CompilerParams(vmem_limit_bytes=PACK_VMEM),
        name="unpack",
    )(turn, *parts)


def attend_kernel(
    slots, list_ref, own, earlier, further, out, query, key, value, counted, result, scores, highest, sems
):
    slab_tiles, _, _, width = own.shape
    window_tiles = slab_tiles + 2 * REACH
    copies = [pltpu.make_async_copy(own.at[:, 0], query, sems.at[0])]
    for source, first, where in (
        (earlier, 0, pl.ds(0, REACH)),
        (own, 1, pl.ds(REACH, slab_tiles)),
        (further, 0, pl.ds(REACH + slab_tiles, REACH)),
    ):
        for which, window in enumerate((key, value)):
            copies.append(
                pltpu.make_async_copy(
                    source.at[:, first + which], window.at[where], sems.at[len(copies)]
                )
            )
    for copy in copies:
        copy.start()
    value[window_tiles] = jnp.zeros((TILE, width), jnp.bfloat16)
    counted[0] = jnp.zeros((TILE, HEAD_DIM), jnp.bfloat16)
    counted[1] = jnp.ones((TILE, HEAD_DIM), jnp.bfloat16)
    for copy in copies:
        copy.wait()
    factor = math.log2(math.e) / math.sqrt(HEAD_DIM)

    def listed(i, head):
        return [list_ref[(head * slab_tiles + i) * slots + j] for j in range(slots)]

    def score(slot, i, head):
        here = pl.ds(head * HEAD_DIM, HEAD_DIM)
        key_from = [jnp.where(n >= 0, n, i + REACH) for n in listed(i, head)]
        tile_queries = query[i, :, here]
        products = []
        for j in range(0, slots, 2):
            both = jnp.concatenate([key[key_from[j], :, here], key[key_from[j + 1], :, here]], axis=0)
            product = lax.dot_general(
                tile_queries, both, (((1,), (1,)), ((), ())), preferred_element_type=jnp.float32
            )
            scores[slot, j // 2] = product
            products.append(product)
        top = jnp.max(functools.reduce(jnp.maximum, products), axis=1, keepdims=True)
        highest[slot] = jnp.broadcast_to(top * factor, (TILE, HEAD_DIM))

    def finish(slot, i, head):
        here = pl.ds(head * HEAD_DIM, HEAD_DIM)
        named = listed(i, head)
        value_from = [jnp.where(n >= 0, n, window_tiles) for n in named]
        ones_from = [jnp.where(n >= 0, 1, 0) for n in named]
        top = jnp.concatenate([highest[slot]] * 2, axis=1)
        weights = [
            jnp.exp2(scores[slot, j] * factor - top).astype(jnp.bfloat16)
            for j in range(slots // 2)
        ]
        summed = jnp.dot(
            jnp.concatenate(weights, axis=1),
            jnp.concatenate(
                [
                    jnp.concatenate([value[v, :, here], counted[o]], axis=1)
                    for v, o in zip(value_from, ones_from)
                ],
                axis=0,
            ),
            preferred_element_type=jnp.float32,
        )
        result[i, :, here] = (summed[:, :HEAD_DIM] / summed[:, HEAD_DIM:]).astype(jnp.bfloat16)

    heads = width // HEAD_DIM
    together = 16 // heads
    steps = [(tile, head) for tile in range(together) for head in range(heads)]
    score(0, 0, 0)

    def some_tiles(n, carry):
        first = n * together
        for number, (tile, head) in enumerate(steps):
            ahead_tile, ahead_head = (steps + [(together, 0)])[number + 1]
            score((number + 1) % 2, jnp.minimum(first + ahead_tile, slab_tiles - 1), ahead_head)
            finish(number % 2, first + tile, head)
        return carry

    lax.fori_loop(0, slab_tiles // together, some_tiles, 0)
    copy = pltpu.make_async_copy(result, out, sems.at[len(copies)])
    copy.start()
    copy.wait()


def attend(lists, own, earlier, further):
    heads, slab_tiles, slots = lists.shape
    window_tiles = slab_tiles + 2 * REACH
    width = heads * HEAD_DIM
    pairs = heads * slab_tiles * slots
    return pl.pallas_call(
        functools.partial(attend_kernel, slots),
        in_specs=[pl.BlockSpec(memory_space=pltpu.SMEM)]
        + [pl.BlockSpec(memory_space=pl.ANY)] * 3,
        out_specs=pl.BlockSpec(memory_space=pl.ANY),
        out_shape=jax.ShapeDtypeStruct((slab_tiles, TILE, width), jnp.bfloat16),
        scratch_shapes=[
            pltpu.VMEM((slab_tiles, TILE, width), jnp.bfloat16),
            pltpu.VMEM((window_tiles, TILE, width), jnp.bfloat16),
            pltpu.VMEM((window_tiles + 1, TILE, width), jnp.bfloat16),
            pltpu.VMEM((2, TILE, HEAD_DIM), jnp.bfloat16),
            pltpu.VMEM((slab_tiles, TILE, width), jnp.bfloat16),
            pltpu.VMEM((2, slots // 2, TILE, 2 * TILE), jnp.float32),
            pltpu.VMEM((2, TILE, HEAD_DIM), jnp.float32),
            pltpu.SemaphoreType.DMA((8,)),
        ],
        compiler_params=pltpu.CompilerParams(vmem_limit_bytes=ATTEND_VMEM),
        cost_estimate=pl.CostEstimate(
            flops=4 * pairs * TILE * TILE * HEAD_DIM,
            bytes_accessed=2 * TILE * width * (2 * slab_tiles + 2 * window_tiles),
            transcendentals=pairs * TILE * TILE,
        ),
        name="attend",
    )(lists.reshape(-1), own, earlier, further)


def on_device(queries, keys, values, key_tiles, tile_mask):
    slab_tiles = key_tiles.shape[1]
    groups = lax.axis_size("uly")
    slab = lax.axis_index("blk")
    turn = flipped(slab, lax.axis_size("blk")).astype(jnp.int32).reshape(1)
    first_tile = slab * slab_tiles - REACH
    lists = jnp.clip(key_tiles - first_tile, 0, slab_tiles + 2 * REACH - 1)
    lists = to_holder(jnp.where(tile_mask > 0, lists, -1))
    received = []
    skipped = 0
    for heads in HEAD_SETS:
        width = heads * HEAD_DIM
        vmem = PACK_VMEM if received else FIRST_PACK_VMEM
        packed = pack((queries, keys, values), turn, groups, skipped, width, vmem)
        skipped += width
        if received:
            packed, received[-1] = lax.optimization_barrier((packed, received[-1]))
        received.append(exchanged(packed))
    results = []
    head = 0
    for heads, own in zip(HEAD_SETS, received):
        earlier = to_neighbour(own[slab_tiles - REACH :, 1:], 1)
        further = to_neighbour(own[:REACH, 1:], -1)
        results.append(exchanged(attend(lists[head : head + heads], own, earlier, further)))
        head += heads
    return unpack(results, turn, groups)


def solution(mesh):
    placed = (
        P(("blk", "uly"), None),
        P(("blk", "uly"), None),
        P(("blk", "uly"), None),
        P("uly", "blk", None),
        P("uly", "blk", None),
    )
    return jax.shard_map(
        on_device, mesh=mesh, in_specs=placed, out_specs=P(("blk", "uly"), None), check_vma=False
    )
```

time: 222 us -> 188 us (0.85)
  blocking collectives: 102 us -> 20.4 us
  waiting for transfers between devices: 34.2 us -> 97.6 us
  Pallas kernels: 44.2 us -> 24.6 us
  starting transfers between devices: 30.7 us -> 34.5 us
    all_to_all x2 -> x1, blocking collectives: 102 us -> 20.4 us  [exchanged(): return lax.all_to_all(x, 'uly', split_axis=0, concat_axis=0, tiled=True)]
    all_to_all x2 -> x3, waiting for transfers between devices: 0.01 us -> 68.6 us  [exchanged(): return lax.all_to_all(x, 'uly', split_axis=0, concat_axis=0, tiled=True)]
    pallas_call x3 -> x4, Pallas kernels: 42.5 us -> 22.9 us  [the longest x2 16.9 us: attend(): pl.pallas_call(functools.partial(attend_kernel, slots), in_specs=[pl.Bloc...]
    ppermute x4 -> x5, waiting for transfers between devices: 34.2 us -> 29 us  [the longest x4 29 us: to_neighbour(): return lax.ppermute(x, ('blk', 'uly'), pairs)]
    ppermute x4 -> x5, starting transfers between devices: 12 us -> 14.1 us  [the longest x4 13.5 us: to_neighbour(): return lax.ppermute(x, ('blk', 'uly'), pairs)]
    all_to_all x2 -> x3, starting transfers between devices: 18.7 us -> 20.4 us  [exchanged(): return lax.all_to_all(x, 'uly', split_axis=0, concat_axis=0, tiled=True)]
    unnamed x12 -> x14, local copies, waits for them, and re-layouts: 5.67 us -> 6.35 us
  transfers between devices with their start and end apart: 6 -> 8, of which waited for: 4 -> 6; matrix products, arithmetic and copies ran while one was open for 2% -> 2% of each run, Pallas kernels for 17% -> 10%
where the time goes in v2:
time: 188 us; the launch traced here: 187 us
  waiting for transfers between devices  97.6 us (52%)
  starting transfers between devices  34.5 us (18%)
  Pallas kernels  24.6 us (13%)
  blocking collectives  20.4 us (11%)
  local copies, waits for them, and re-layouts  9.25 us (5%)
    all_to_all x3, waiting for transfers between devices, exchanged(): return lax.all_to_all(x, 'uly', split_axis=0, concat_axis=0, tiled=True)  68.6 us
    ppermute x4, waiting for transfers between devices, to_neighbour(): return lax.ppermute(x, ('blk', 'uly'), pairs)  29 us
    all_to_all x3, starting transfers between devices, exchanged(): return lax.all_to_all(x, 'uly', split_axis=0, concat_axis=0, tiled=True)  20.4 us
    all_to_all x1, blocking collectives, exchanged(): return lax.all_to_all(x, 'uly', split_axis=0, concat_axis=0, tiled=True)  20.4 us
    pallas_call x2, Pallas kernels, attend(): pl.pallas_call(functools.partial(attend_kernel, slots), in_specs=[pl.Bloc...  16.9 us
    ppermute x4, starting transfers between devices, to_neighbour(): return lax.ppermute(x, ('blk', 'uly'), pairs)  13.5 us
    unnamed x14, local copies, waits for them, and re-layouts  6.35 us
    pallas_call x2, Pallas kernels, pack(): pl.pallas_call(functools.partial(pack_kernel, columns // groups, skipped,...  5.96 us
  transfers between devices with their start and end apart: 8, of which 6 were waited for; matrix products, arithmetic and copies ran while one was open for 2% of the time, Pallas kernels for 10%

profile of v2, /device:TPU:7, one launch (start us, length us, event | category | flops | bytes accessed | tf_op | source)
XLA Modules:
  0.0 186.6 jit_solution(9658911480183773832)
XLA Ops:
  0.0 4.4 %pack.3 = bf16[16,3,128,256]{3,2,1,0:T(8,128)(2,1)} custom-call(s32[1]{0:T(128)} %bitcast.turn_ref, bf16[128,6144]{1,0:T(8,128)(2,1)} %refs_0_.3, bf16[128,6144]{1,0:T(8,128)(2,1)} %refs_1_.3, bf16[128,6144]{1,0:T(8,128)(2,1)} %refs_2_.3), custom_call_target="tpu_custom_call" | custom-call | bytes 7864320 | tf_op jit(solution)/shard_map/pack/pallas_call | solution.py:81
  4.4 9.3 %all-to-all-start = ((bf16[16,3,128,256]{3,2,1,0:T(8,128)(2,1)}), bf16[16,3,128,256]{3,2,1,0:T(8,128)(2,1)S(1)}, u32[]{:S(2)}, u32[]{:S(2)}) async-start(bf16[16,3,128,256]{3,2,1,0:T(8,128)(2,1)} %pack.3), calls=%async_computation | async-start | bytes 6291456 | tf_op jit(solution)/shard_map/all_to_all | solution.py:47
  13.7 1.4 copy-done.1
  15.1 1.4 copy-done.2
  16.5 1.4 copy-done.3
  17.9 1.6 pack.2
  20.7 65.6 %all-to-all-done.own = bf16[16,3,128,256]{3,2,1,0:T(8,128)(2,1)S(1)} async-done(((bf16[16,3,128,256]{3,2,1,0:T(8,128)(2,1)}), bf16[16,3,128,256]{3,2,1,0:T(8,128)(2,1)S(1)}, u32[]{:S(2)}, u32[]{:S(2)}) %all-to-all-start) | async-done | bytes 3145760 | tf_op jit(solution)/shard_map/all_to_all | solution.py:47
  86.3 4.4 %all-to-all-start.2 = ((bf16[16,3,128,128]{3,2,1,0:T(8,128)(2,1)}), bf16[16,3,128,128]{3,2,1,0:T(8,128)(2,1)}, u32[]{:S(2)}, u32[]{:S(2)}) async-start(bf16[16,3,128,128]{3,2,1,0:T(8,128)(2,1)} %copy-done), calls=%async_computation.2 | async-start | bytes 3145728 | tf_op jit(solution)/shard_map/all_to_all | solution.py:47
  90.8 1.4 fusion
  92.2 6.4 %collective-permute-start.1 = (bf16[8,2,128,256]{3,2,1,0:T(8,128)(2,1)}, bf16[8,2,128,256]{3,2,1,0:T(8,128)(2,1)}, u32[]{:S(2)}, u32[]{:S(2)}) collective-permute-start(bf16[8,2,128,256]{3,2,1,0:T(8,128)(2,1)} %get-tuple-element.10), channel_id=1, source_target_pairs={{0,16},{1,17},{2,18},{3,19},{4,20},{5,21},{6,22},{7,23},{8,24},{9,... | collective-permute-start | bytes 3145736 | tf_op jit(solution)/shard_map/ppermute | solution.py:33
  98.5 1.9 %collective-permute-start.2 = (bf16[8,2,128,256]{3,2,1,0:T(8,128)(2,1)}, bf16[8,2,128,256]{3,2,1,0:T(8,128)(2,1)}, u32[]{:S(2)}, u32[]{:S(2)}) collective-permute-start(bf16[8,2,128,256]{3,2,1,0:T(8,128)(2,1)} %get-tuple-element.9), channel_id=1, source_target_pairs={{16,0},{17,1},{18,2},{19,3},{20,4},{21,5},{22,6},{23,7},{24,8},{25... | collective-permute-start | bytes 3145736 | tf_op jit(solution)/shard_map/ppermute | solution.py:33
  101.3 9.3 %collective-permute-done.1.earlier = bf16[8,2,128,256]{3,2,1,0:T(8,128)(2,1)} collective-permute-done((bf16[8,2,128,256]{3,2,1,0:T(8,128)(2,1)}, bf16[8,2,128,256]{3,2,1,0:T(8,128)(2,1)}, u32[]{:S(2)}, u32[]{:S(2)}) %collective-permute-start.1) | collective-permute-done | bytes 1048608 | tf_op jit(solution)/shard_map/ppermute | solution.py:33
  110.6 7.9 %collective-permute-done.2.further = bf16[8,2,128,256]{3,2,1,0:T(8,128)(2,1)} collective-permute-done((bf16[8,2,128,256]{3,2,1,0:T(8,128)(2,1)}, bf16[8,2,128,256]{3,2,1,0:T(8,128)(2,1)}, u32[]{:S(2)}, u32[]{:S(2)}) %collective-permute-start.2) | collective-permute-done | bytes 1048608 | tf_op jit(solution)/shard_map/ppermute | solution.py:33
  118.4 10.6 %attend.2 = bf16[16,128,256]{2,1,0:T(8,128)(2,1)S(1)} custom-call(s32[384]{0:T(512)S(1)} %reshape.10.list_ref, bf16[16,3,128,256]{3,2,1,0:T(8,128)(2,1)S(1)} %all-to-all-done.own, bf16[8,2,128,256]{3,2,1,0:T(8,128)(2,1)} %collective-permute-done.1.earlier, bf16[8,2,128,256]{3,2,1,0:T(8,128)(2,1)} %collective-permute-done.2.further), custom_call_target="tpu_custom_call" | custom-call | flops 3221225472 | bytes 6291456 | tf_op jit(solution)/shard_map/attend/pallas_call | solution.py:217
  130.0 6.7 %all-to-all-start.1 = ((bf16[16,128,256]{2,1,0:T(8,128)(2,1)}), bf16[16,128,256]{2,1,0:T(8,128)(2,1)S(1)}, u32[]{:S(2)}, u32[]{:S(2)}) async-start(bf16[16,128,256]{2,1,0:T(8,128)(2,1)} %copy-done.4), calls=%async_computation.1 | async-start | bytes 2097152 | tf_op jit(solution)/shard_map/all_to_all | solution.py:47
  136.7 1.3 fusion.1
  138.0 3.1 %collective-permute-start.3 = (bf16[8,2,128,128]{3,2,1,0:T(8,128)(2,1)S(1)}, bf16[8,2,128,128]{3,2,1,0:T(8,128)(2,1)S(1)}, u32[]{:S(2)}, u32[]{:S(2)}) collective-permute-start(bf16[8,2,128,128]{3,2,1,0:T(8,128)(2,1)S(1)} %get-tuple-element.12), channel_id=1, source_target_pairs={{0,16},{1,17},{2,18},{3,19},{4,20},{5,21},{6,22},{7,23},{8,24},{9,... | collective-permute-start | bytes 1572872 | tf_op jit(solution)/shard_map/ppermute | solution.py:33
  141.1 2.1 %collective-permute-start.4 = (bf16[8,2,128,128]{3,2,1,0:T(8,128)(2,1)S(1)}, bf16[8,2,128,128]{3,2,1,0:T(8,128)(2,1)S(1)}, u32[]{:S(2)}, u32[]{:S(2)}) collective-permute-start(bf16[8,2,128,128]{3,2,1,0:T(8,128)(2,1)S(1)} %get-tuple-element.11), channel_id=1, source_target_pairs={{16,0},{17,1},{18,2},{19,3},{20,4},{21,5},{22,6},{23,7},{24,8},{25... | collective-permute-start | bytes 1572872 | tf_op jit(solution)/shard_map/ppermute | solution.py:33
  143.3 3.9 %collective-permute-done.3.earlier = bf16[8,2,128,128]{3,2,1,0:T(8,128)(2,1)S(1)} collective-permute-done((bf16[8,2,128,128]{3,2,1,0:T(8,128)(2,1)S(1)}, bf16[8,2,128,128]{3,2,1,0:T(8,128)(2,1)S(1)}, u32[]{:S(2)}, u32[]{:S(2)}) %collective-permute-start.3) | collective-permute-done | bytes 524320 | tf_op jit(solution)/shard_map/ppermute | solution.py:33
  147.2 8.0 %collective-permute-done.4.further = bf16[8,2,128,128]{3,2,1,0:T(8,128)(2,1)S(1)} collective-permute-done((bf16[8,2,128,128]{3,2,1,0:T(8,128)(2,1)S(1)}, bf16[8,2,128,128]{3,2,1,0:T(8,128)(2,1)S(1)}, u32[]{:S(2)}, u32[]{:S(2)}) %collective-permute-start.4) | collective-permute-done | bytes 524320 | tf_op jit(solution)/shard_map/ppermute | solution.py:33
  155.2 6.3 %attend.3 = bf16[16,128,128]{2,1,0:T(8,128)(2,1)S(1)} custom-call(s32[192]{0:T(256)S(1)} %reshape.11.list_ref, bf16[16,3,128,128]{3,2,1,0:T(8,128)(2,1)} %all-to-all-done.2.own, bf16[8,2,128,128]{3,2,1,0:T(8,128)(2,1)S(1)} %collective-permute-done.3.earlier, bf16[8,2,128,128]{3,2,1,0:T(8,128)(2,1)S(1)} %collective-permute-done.4.further), custom_call_target="tpu_custom_call" | custom-call | flops 1610612736 | bytes 3145728 | tf_op jit(solution)/shard_map/attend/pallas_call | solution.py:217
  161.6 3.0 %all-to-all-done.1.refs_0_ = bf16[16,128,256]{2,1,0:T(8,128)(2,1)S(1)} async-done(((bf16[16,128,256]{2,1,0:T(8,128)(2,1)}), bf16[16,128,256]{2,1,0:T(8,128)(2,1)S(1)}, u32[]{:S(2)}, u32[]{:S(2)}) %all-to-all-start.1) | async-done | bytes 1048608 | tf_op jit(solution)/shard_map/all_to_all | solution.py:47
  164.5 20.4 %all_to_all.20.refs_1_ = bf16[16,128,128]{2,1,0:T(8,128)(2,1)S(1)} all-to-all(bf16[16,128,128]{2,1,0:T(8,128)(2,1)S(1)} %attend.3), channel_id=1, replica_groups=mesh['blk'=16,'uly'=16] {'uly'}, dimensions={0} | all-to-all | bytes 1048576 | tf_op jit(solution)/shard_map/all_to_all | solution.py:47
  184.9 1.7 unpack.1
  (19 shorter events, 3.0 us)
Async XLA Ops:
  4.4 81.9 %all-to-all-start = ((bf16[16,3,128,256]{3,2,1,0:T(8,128)(2,1)}), bf16[16,3,128,256]{3,2,1,0:T(8,128)(2,1)S(1)}, u32[]{:S(2)}, u32[]{:S(2)}) async-start(bf16[16,3,128,256]{3,2,1,0:T(8,128)(2,1)} %pack.3), calls=%async_computation | async-start | bytes 6291456 | tf_op jit(solution)/shard_map/all_to_all | solution.py:47
  13.7 1.4 copy-start.1
  15.1 1.4 copy-start.2
  16.5 1.4 copy-start.3
  19.5 1.1 copy-start
  86.3 43.7 %all-to-all-start.2 = ((bf16[16,3,128,128]{3,2,1,0:T(8,128)(2,1)}), bf16[16,3,128,128]{3,2,1,0:T(8,128)(2,1)}, u32[]{:S(2)}, u32[]{:S(2)}) async-start(bf16[16,3,128,128]{3,2,1,0:T(8,128)(2,1)} %copy-done), calls=%async_computation.2 | async-start | bytes 3145728 | tf_op jit(solution)/shard_map/all_to_all | solution.py:47
  90.7 9.8 %copy-start.5 = (s32[3,16,12]{2,1,0:T(8,128)S(1)}, s32[3,16,12]{2,1,0:T(8,128)}, u32[]{:S(2)}) copy-start(s32[3,16,12]{2,1,0:T(8,128)} %param.8) | copy-start | bytes 6916
  90.7 9.8 %copy-start.6 = (s32[3,16,12]{2,1,0:T(8,128)S(1)}, s32[3,16,12]{2,1,0:T(8,128)}, u32[]{:S(2)}) copy-start(s32[3,16,12]{2,1,0:T(8,128)} %param.9) | copy-start | bytes 6916
  92.2 18.4 %collective-permute-start.1 = (bf16[8,2,128,256]{3,2,1,0:T(8,128)(2,1)}, bf16[8,2,128,256]{3,2,1,0:T(8,128)(2,1)}, u32[]{:S(2)}, u32[]{:S(2)}) collective-permute-start(bf16[8,2,128,256]{3,2,1,0:T(8,128)(2,1)} %get-tuple-element.10), channel_id=1, source_target_pairs={{0,16},{1,17},{2,18},{3,19},{4,20},{5,21},{6,22},{7,23},{8,24},{9,... | collective-permute-start | bytes 3145736 | tf_op jit(solution)/shard_map/ppermute | solution.py:33
  98.5 19.9 %collective-permute-start.2 = (bf16[8,2,128,256]{3,2,1,0:T(8,128)(2,1)}, bf16[8,2,128,256]{3,2,1,0:T(8,128)(2,1)}, u32[]{:S(2)}, u32[]{:S(2)}) collective-permute-start(bf16[8,2,128,256]{3,2,1,0:T(8,128)(2,1)} %get-tuple-element.9), channel_id=1, source_target_pairs={{16,0},{17,1},{18,2},{19,3},{20,4},{21,5},{22,6},{23,7},{24,8},{25... | collective-permute-start | bytes 3145736 | tf_op jit(solution)/shard_map/ppermute | solution.py:33
  100.5 0.7 collective-permute-start
  129.0 1.0 copy-start.4
  130.0 34.5 %all-to-all-start.1 = ((bf16[16,128,256]{2,1,0:T(8,128)(2,1)}), bf16[16,128,256]{2,1,0:T(8,128)(2,1)S(1)}, u32[]{:S(2)}, u32[]{:S(2)}) async-start(bf16[16,128,256]{2,1,0:T(8,128)(2,1)} %copy-done.4), calls=%async_computation.1 | async-start | bytes 2097152 | tf_op jit(solution)/shard_map/all_to_all | solution.py:47
  138.0 9.2 %collective-permute-start.3 = (bf16[8,2,128,128]{3,2,1,0:T(8,128)(2,1)S(1)}, bf16[8,2,128,128]{3,2,1,0:T(8,128)(2,1)S(1)}, u32[]{:S(2)}, u32[]{:S(2)}) collective-permute-start(bf16[8,2,128,128]{3,2,1,0:T(8,128)(2,1)S(1)} %get-tuple-element.12), channel_id=1, source_target_pairs={{0,16},{1,17},{2,18},{3,19},{4,20},{5,21},{6,22},{7,23},{8,24},{9,... | collective-permute-start | bytes 1572872 | tf_op jit(solution)/shard_map/ppermute | solution.py:33
  141.1 14.1 %collective-permute-start.4 = (bf16[8,2,128,128]{3,2,1,0:T(8,128)(2,1)S(1)}, bf16[8,2,128,128]{3,2,1,0:T(8,128)(2,1)S(1)}, u32[]{:S(2)}, u32[]{:S(2)}) collective-permute-start(bf16[8,2,128,128]{3,2,1,0:T(8,128)(2,1)S(1)} %get-tuple-element.11), channel_id=1, source_target_pairs={{16,0},{17,1},{18,2},{19,3},{20,4},{21,5},{22,6},{23,7},{24,8},{25... | collective-permute-start | bytes 1572872 | tf_op jit(solution)/shard_map/ppermute | solution.py:33

commit v3 on v2

--- a/solution.py
+++ b/solution.py
@@ -47,23 +47,19 @@
     return lax.all_to_all(x, "uly", split_axis=0, concat_axis=0, tiled=True)
 
 
-def pack_kernel(per_group, skipped, chunks, turn_ref, *refs):
+def pack_kernel(per_group, skipped, turn_ref, *refs):
     inputs, (out, held, arrived, left) = refs[:3], refs[3:]
     groups, width = out.shape[0], out.shape[-1]
-    per_chunk = groups // chunks
-    span = per_chunk * per_group
-    taken, sent = [], []
-    for chunk in range(chunks):
-        for which, ref in enumerate(inputs):
-            here = pl.ds(chunk * span, span)
-            copy = pltpu.make_async_copy(
-                ref.at[:, here], held.at[which, :, here], arrived.at[which, chunk]
-            )
-            copy.start()
-            taken.append((chunk, which, copy))
-    for chunk, which, copy in taken:
+    taken = [
+        pltpu.make_async_copy(ref, held.at[which], arrived.at[which])
+        for which, ref in enumerate(inputs)
+    ]
+    for copy in taken:
+        copy.start()
+    sent = []
+    for which, copy in enumerate(taken):
         copy.wait()
-        for group in range(chunk * per_chunk, (chunk + 1) * per_chunk):
+        for group in range(groups):
             copy = pltpu.make_async_copy(
                 held.at[which, :, pl.ds(group * per_group + skipped, width)],
                 out.at[group ^ turn_ref[0], which],
@@ -76,17 +72,16 @@
 
 
 def pack(inputs, turn, groups, skipped, width, vmem):
-    chunks = 4
     rows, columns = inputs[0].shape
     return pl.pallas_call(
-        functools.partial(pack_kernel, columns // groups, skipped, chunks),
+        functools.partial(pack_kernel, columns // groups, skipped),
         in_specs=[pl.BlockSpec(memory_space=pltpu.SMEM)]
         + [pl.BlockSpec(memory_space=pltpu.HBM)] * 3,
         out_specs=pl.BlockSpec(memory_space=pltpu.HBM),
         out_shape=jax.ShapeDtypeStruct((groups, 3, rows, width), jnp.bfloat16),
         scratch_shapes=[
             pltpu.VMEM((3, rows, columns), jnp.bfloat16),
-            pltpu.SemaphoreType.DMA((3, chunks)),
+            pltpu.SemaphoreType.DMA((3,)),
             pltpu.SemaphoreType.DMA((3, groups)),
         ],
         compiler_params=pltpu.CompilerParams(vmem_limit_bytes=vmem),
@@ -123,16 +118,16 @@
     )(turn, *parts)
 
 
-def attend_kernel(
-    slots, list_ref, own, earlier, further, out, query, key, value, counted, result, scores, highest, sems
-):
+def attend_kernel(first_tile, tiles, slots, n_filled, list_ref, own, halo, *refs):
+    out, query, key, value, counted, result, scores, highest, sems = refs[n_filled:]
     slab_tiles, _, _, width = own.shape
-    window_tiles = slab_tiles + 2 * REACH
-    copies = [pltpu.make_async_copy(own.at[:, 0], query, sems.at[0])]
+    window_tiles = slab_tiles + REACH
+    halo_at, own_at = (0, REACH) if first_tile == 0 else (slab_tiles, 0)
+    centre = first_tile + own_at
+    copies = [pltpu.make_async_copy(own.at[pl.ds(first_tile, tiles), 0], query, sems.at[0])]
     for source, first, where in (
-        (earlier, 0, pl.ds(0, REACH)),
-        (own, 1, pl.ds(REACH, slab_tiles)),
-        (further, 0, pl.ds(REACH + slab_tiles, REACH)),
+        (halo, 0, pl.ds(halo_at, REACH)),
+        (own, 1, pl.ds(own_at, slab_tiles)),
     ):
         for which, window in enumerate((key, value)):
             copies.append(
@@ -150,11 +145,11 @@
     factor = math.log2(math.e) / math.sqrt(HEAD_DIM)
 
     def listed(i, head):
-        return [list_ref[(head * slab_tiles + i) * slots + j] for j in range(slots)]
+        return [list_ref[(head * tiles + i) * slots + j] for j in range(slots)]
 
     def score(slot, i, head):
         here = pl.ds(head * HEAD_DIM, HEAD_DIM)
-        key_from = [jnp.where(n >= 0, n, i + REACH) for n in listed(i, head)]
+        key_from = [jnp.where(n >= 0, n, i + centre) for n in listed(i, head)]
         tile_queries = query[i, :, here]
         products = []
         for j in range(0, slots, 2):
@@ -191,7 +186,7 @@
         result[i, :, here] = (summed[:, :HEAD_DIM] / summed[:, HEAD_DIM:]).astype(jnp.bfloat16)
 
     heads = width // HEAD_DIM
-    together = 16 // heads
+    together = tiles
     steps = [(tile, head) for tile in range(together) for head in range(heads)]
     score(0, 0, 0)
 
@@ -199,54 +194,60 @@
         first = n * together
         for number, (tile, head) in enumerate(steps):
             ahead_tile, ahead_head = (steps + [(together, 0)])[number + 1]
-            score((number + 1) % 2, jnp.minimum(first + ahead_tile, slab_tiles - 1), ahead_head)
+            score((number + 1) % 2, jnp.minimum(first + ahead_tile, tiles - 1), ahead_head)
             finish(number % 2, first + tile, head)
         return carry
 
-    lax.fori_loop(0, slab_tiles // together, some_tiles, 0)
-    copy = pltpu.make_async_copy(result, out, sems.at[len(copies)])
+    lax.fori_loop(0, tiles // together, some_tiles, 0)
+    copy = pltpu.make_async_copy(
+        result, out.at[pl.ds(first_tile, tiles)], sems.at[len(copies)]
+    )
     copy.start()
     copy.wait()
 
 
-def attend(lists, own, earlier, further):
-    heads, slab_tiles, slots = lists.shape
-    window_tiles = slab_tiles + 2 * REACH
+def attend(lists, first_tile, own, halo, filled=()):
+    heads, tiles, slots = lists.shape
+    slab_tiles = own.shape[0]
+    window_tiles = slab_tiles + REACH
     width = heads * HEAD_DIM
-    pairs = heads * slab_tiles * slots
+    pairs = heads * tiles * slots
     return pl.pallas_call(
-        functools.partial(attend_kernel, slots),
+        functools.partial(attend_kernel, first_tile, tiles, slots, len(filled)),
         in_specs=[pl.BlockSpec(memory_space=pltpu.SMEM)]
-        + [pl.BlockSpec(memory_space=pl.ANY)] * 3,
+        + [pl.BlockSpec(memory_space=pl.ANY)] * (2 + len(filled)),
         out_specs=pl.BlockSpec(memory_space=pl.ANY),
         out_shape=jax.ShapeDtypeStruct((slab_tiles, TILE, width), jnp.bfloat16),
         scratch_shapes=[
-            pltpu.VMEM((slab_tiles, TILE, width), jnp.bfloat16),
+            pltpu.VMEM((tiles, TILE, width), jnp.bfloat16),
             pltpu.VMEM((window_tiles, TILE, width), jnp.bfloat16),
             pltpu.VMEM((window_tiles + 1, TILE, width), jnp.bfloat16),
             pltpu.VMEM((2, TILE, HEAD_DIM), jnp.bfloat16),
-            pltpu.VMEM((slab_tiles, TILE, width), jnp.bfloat16),
+            pltpu.VMEM((tiles, TILE, width), jnp.bfloat16),
             pltpu.VMEM((2, slots // 2, TILE, 2 * TILE), jnp.float32),
             pltpu.VMEM((2, TILE, HEAD_DIM), jnp.float32),
-            pltpu.SemaphoreType.DMA((8,)),
+            pltpu.SemaphoreType.DMA((6,)),
         ],
+        input_output_aliases={3: 0} if filled else {},
         compiler_params=pltpu.CompilerParams(vmem_limit_bytes=ATTEND_VMEM),
         cost_estimate=pl.CostEstimate(
             flops=4 * pairs * TILE * TILE * HEAD_DIM,
-            bytes_accessed=2 * TILE * width * (2 * slab_tiles + 2 * window_tiles),
+            bytes_accessed=2 * TILE * width * (2 * tiles + 2 * window_tiles),
             transcendentals=pairs * TILE * TILE,
         ),
         name="attend",
-    )(lists.reshape(-1), own, earlier, further)
+    )(lists.reshape(-1), own, halo, *filled)
 
 
 def on_device(queries, keys, values, key_tiles, tile_mask):
     slab_tiles = key_tiles.shape[1]
+    half = slab_tiles // 2
     groups = lax.axis_size("uly")
     slab = lax.axis_index("blk")
     turn = flipped(slab, lax.axis_size("blk")).astype(jnp.int32).reshape(1)
-    first_tile = slab * slab_tiles - REACH
-    lists = jnp.clip(key_tiles - first_tile, 0, slab_tiles + 2 * REACH - 1)
+    lower = jnp.arange(slab_tiles)[:, None] < half
+    window_start = slab * slab_tiles - jnp.where(lower, REACH, 0)
+    lists = jnp.clip(key_tiles - window_start, 0, slab_tiles + REACH - 1)
     lists = to_holder(jnp.where(tile_mask > 0, lists, -1))
     received = []
     skipped = 0
@@ -256,14 +257,17 @@
         packed = pack((queries, keys, values), turn, groups, skipped, width, vmem)
         skipped += width
         if received:
-            packed, received[-1] = lax.optimization_barrier((packed, received[-1]))
+            packed, received[-1], lists = lax.optimization_barrier((packed, received[-1], lists))
         received.append(exchanged(packed))
     results = []
     head = 0
     for heads, own in zip(HEAD_SETS, received):
+        here = lists[head : head + heads]
         earlier = to_neighbour(own[slab_tiles - REACH :, 1:], 1)
         further = to_neighbour(own[:REACH, 1:], -1)
-        results.append(exchanged(attend(lists[head : head + heads], own, earlier, further)))
+        attended = attend(here[:, :half], 0, own, earlier)
+        attended = attend(here[:, half:], half, own, further, (attended,))
+        results.append(exchanged(attended))
         head += heads
     return unpack(results, turn, groups)
 

time: 188 us -> 186 us (0.989)
  waiting for transfers between devices: 97.6 us -> 83.5 us
  starting transfers between devices: 34.5 us -> 39.4 us
  Pallas kernels: 24.6 us -> 28.8 us
  blocking collectives: 20.4 us -> 24.2 us
    ppermute x4, waiting for transfers between devices: 29 us -> 18.3 us  [to_neighbour(): return lax.ppermute(x, ('blk', 'uly'), pairs)]
    pallas_call x4 -> x6, Pallas kernels: 22.9 us -> 27.1 us  [the longest x4 22 us: attend(): pl.pallas_call(functools.partial(attend_kernel, first_tile, tiles, slots,...]
    ppermute x4, starting transfers between devices: 13.5 us -> 17.6 us  [to_neighbour(): return lax.ppermute(x, ('blk', 'uly'), pairs)]
    all_to_all x1, blocking collectives: 20.4 us -> 24.2 us  [exchanged(): return lax.all_to_all(x, 'uly', split_axis=0, concat_axis=0, tiled=True)]
    all_to_all x3, waiting for transfers between devices: 68.6 us -> 65.2 us  [exchanged(): return lax.all_to_all(x, 'uly', split_axis=0, concat_axis=0, tiled=True)]
  transfers between devices with their start and end apart: 8 -> 8, of which waited for: 6 -> 6; matrix products, arithmetic and copies ran while one was open for 2% -> 2% of each run, Pallas kernels for 10% -> 13%
where the time goes in v3:
time: 186 us
  waiting for transfers between devices  83.5 us (45%)
  starting transfers between devices  39.4 us (21%)
  Pallas kernels  28.8 us (15%)
  blocking collectives  24.2 us (13%)
  local copies, waits for them, and re-layouts  9.39 us (5%)
    all_to_all x3, waiting for transfers between devices, exchanged(): return lax.all_to_all(x, 'uly', split_axis=0, concat_axis=0, tiled=True)  65.2 us
    all_to_all x1, blocking collectives, exchanged(): return lax.all_to_all(x, 'uly', split_axis=0, concat_axis=0, tiled=True)  24.2 us
    pallas_call x4, Pallas kernels, attend(): pl.pallas_call(functools.partial(attend_kernel, first_tile, tiles, slots,...  22 us
    all_to_all x3, starting transfers between devices, exchanged(): return lax.all_to_all(x, 'uly', split_axis=0, concat_axis=0, tiled=True)  21.1 us
    ppermute x4, waiting for transfers between devices, to_neighbour(): return lax.ppermute(x, ('blk', 'uly'), pairs)  18.3 us
    ppermute x4, starting transfers between devices, to_neighbour(): return lax.ppermute(x, ('blk', 'uly'), pairs)  17.6 us
    unnamed x14, local copies, waits for them, and re-layouts  6.34 us
    pallas_call x2, Pallas kernels, pack(): pl.pallas_call(functools.partial(pack_kernel, columns // groups, skipped)...  5.1 us
  transfers between devices with their start and end apart: 8, of which 6 were waited for; matrix products, arithmetic and copies ran while one was open for 2% of the time, Pallas kernels for 13%

profile of v3, /device:TPU:7, one launch (start us, length us, event | category | flops | bytes accessed | tf_op | source)
XLA Modules:
  0.0 185.6 jit_solution(913498931117101549)
XLA Ops:
  0.0 3.8 %pack.3 = bf16[16,3,128,256]{3,2,1,0:T(8,128)(2,1)} custom-call(s32[1]{0:T(128)} %bitcast.turn_ref, bf16[128,6144]{1,0:T(8,128)(2,1)} %refs_0_.3, bf16[128,6144]{1,0:T(8,128)(2,1)} %refs_1_.3, bf16[128,6144]{1,0:T(8,128)(2,1)} %refs_2_.3), custom_call_target="tpu_custom_call" | custom-call | bytes 7864320 | tf_op jit(solution)/shard_map/pack/pallas_call | solution.py:76
  3.8 9.3 %all-to-all-start = ((bf16[16,3,128,256]{3,2,1,0:T(8,128)(2,1)}), bf16[16,3,128,256]{3,2,1,0:T(8,128)(2,1)S(1)}, u32[]{:S(2)}, u32[]{:S(2)}) async-start(bf16[16,3,128,256]{3,2,1,0:T(8,128)(2,1)} %pack.3), calls=%async_computation | async-start | bytes 6291456 | tf_op jit(solution)/shard_map/all_to_all | solution.py:47
  13.9 1.4 copy-done.1
  15.3 1.4 copy-done.2
  16.7 1.4 copy-done.3
  18.2 1.3 pack.2
  20.6 65.1 %all-to-all-done.own = bf16[16,3,128,256]{3,2,1,0:T(8,128)(2,1)S(1)} async-done(((bf16[16,3,128,256]{3,2,1,0:T(8,128)(2,1)}), bf16[16,3,128,256]{3,2,1,0:T(8,128)(2,1)S(1)}, u32[]{:S(2)}, u32[]{:S(2)}) %all-to-all-start) | async-done | bytes 3145760 | tf_op jit(solution)/shard_map/all_to_all | solution.py:47
  85.8 4.4 %all-to-all-start.2 = ((bf16[16,3,128,128]{3,2,1,0:T(8,128)(2,1)}), bf16[16,3,128,128]{3,2,1,0:T(8,128)(2,1)}, u32[]{:S(2)}, u32[]{:S(2)}) async-start(bf16[16,3,128,128]{3,2,1,0:T(8,128)(2,1)} %copy-done), calls=%async_computation.2 | async-start | bytes 3145728 | tf_op jit(solution)/shard_map/all_to_all | solution.py:47
  90.2 1.4 fusion.1
  91.6 6.4 %collective-permute-start.2 = (bf16[8,2,128,256]{3,2,1,0:T(8,128)(2,1)}, bf16[8,2,128,256]{3,2,1,0:T(8,128)(2,1)}, u32[]{:S(2)}, u32[]{:S(2)}) collective-permute-start(bf16[8,2,128,256]{3,2,1,0:T(8,128)(2,1)} %get-tuple-element.11), channel_id=1, source_target_pairs={{0,16},{1,17},{2,18},{3,19},{4,20},{5,21},{6,22},{7,23},{8,24},{9,... | collective-permute-start | bytes 3145736 | tf_op jit(solution)/shard_map/ppermute | solution.py:33
  98.0 1.9 %collective-permute-start.1 = (bf16[8,2,128,256]{3,2,1,0:T(8,128)(2,1)}, bf16[8,2,128,256]{3,2,1,0:T(8,128)(2,1)}, u32[]{:S(2)}, u32[]{:S(2)}) collective-permute-start(bf16[8,2,128,256]{3,2,1,0:T(8,128)(2,1)} %get-tuple-element.12), channel_id=1, source_target_pairs={{16,0},{17,1},{18,2},{19,3},{20,4},{21,5},{22,6},{23,7},{24,8},{25... | collective-permute-start | bytes 3145736 | tf_op jit(solution)/shard_map/ppermute | solution.py:33
  100.1 9.9 %collective-permute-done.2.halo = bf16[8,2,128,256]{3,2,1,0:T(8,128)(2,1)} collective-permute-done((bf16[8,2,128,256]{3,2,1,0:T(8,128)(2,1)}, bf16[8,2,128,256]{3,2,1,0:T(8,128)(2,1)}, u32[]{:S(2)}, u32[]{:S(2)}) %collective-permute-start.2) | collective-permute-done | bytes 1048608 | tf_op jit(solution)/shard_map/ppermute | solution.py:33
  110.0 6.7 %attend.4.refs_0_ = bf16[16,128,256]{2,1,0:T(8,128)(2,1)S(1)} custom-call(s32[192]{0:T(256)S(1)} %reshape.27.list_ref, bf16[16,3,128,256]{3,2,1,0:T(8,128)(2,1)S(1)} %all-to-all-done.own, bf16[8,2,128,256]{3,2,1,0:T(8,128)(2,1)} %collective-permute-done.2.halo), custom_call_target="tpu_custom_call" | custom-call | flops 1610612736 | bytes 4194304 | tf_op jit(solution)/shard_map/attend/pallas_call | solution.py:215
  117.9 6.7 %attend.5 = bf16[16,128,256]{2,1,0:T(8,128)(2,1)S(1)} custom-call(s32[192]{0:T(256)S(1)} %reshape.26.list_ref, bf16[16,3,128,256]{3,2,1,0:T(8,128)(2,1)S(1)} %all-to-all-done.own, bf16[8,2,128,256]{3,2,1,0:T(8,128)(2,1)} %collective-permute-done.1.halo, bf16[16,128,256]{2,1,0:T(8,128)(2,1)S(1)} %attend.4.refs_0_), custom_call_target="tpu_custom_call", output_to_operand_aliasing={{}: (3, {})} | custom-call | flops 1610612736 | bytes 4194304 | tf_op jit(solution)/shard_map/attend/pallas_call | solution.py:215
  125.6 7.4 %all-to-all-start.1 = ((bf16[16,128,256]{2,1,0:T(8,128)(2,1)}), bf16[16,128,256]{2,1,0:T(8,128)(2,1)S(1)}, u32[]{:S(2)}, u32[]{:S(2)}) async-start(bf16[16,128,256]{2,1,0:T(8,128)(2,1)} %copy-done.4), calls=%async_computation.1 | async-start | bytes 2097152 | tf_op jit(solution)/shard_map/all_to_all | solution.py:47
  133.1 1.3 fusion.2
  134.3 7.2 %collective-permute-start.4 = (bf16[8,2,128,128]{3,2,1,0:T(8,128)(2,1)S(1)}, bf16[8,2,128,128]{3,2,1,0:T(8,128)(2,1)S(1)}, u32[]{:S(2)}, u32[]{:S(2)}) collective-permute-start(bf16[8,2,128,128]{3,2,1,0:T(8,128)(2,1)S(1)} %get-tuple-element.13), channel_id=1, source_target_pairs={{0,16},{1,17},{2,18},{3,19},{4,20},{5,21},{6,22},{7,23},{8,24},{9,... | collective-permute-start | bytes 1572872 | tf_op jit(solution)/shard_map/ppermute | solution.py:33
  141.6 2.1 %collective-permute-start.3 = (bf16[8,2,128,128]{3,2,1,0:T(8,128)(2,1)S(1)}, bf16[8,2,128,128]{3,2,1,0:T(8,128)(2,1)S(1)}, u32[]{:S(2)}, u32[]{:S(2)}) collective-permute-start(bf16[8,2,128,128]{3,2,1,0:T(8,128)(2,1)S(1)} %get-tuple-element.14), channel_id=1, source_target_pairs={{16,0},{17,1},{18,2},{19,3},{20,4},{21,5},{22,6},{23,7},{24,8},{25... | collective-permute-start | bytes 1572872 | tf_op jit(solution)/shard_map/ppermute | solution.py:33
  143.9 3.8 %collective-permute-done.4.halo = bf16[8,2,128,128]{3,2,1,0:T(8,128)(2,1)S(1)} collective-permute-done((bf16[8,2,128,128]{3,2,1,0:T(8,128)(2,1)S(1)}, bf16[8,2,128,128]{3,2,1,0:T(8,128)(2,1)S(1)}, u32[]{:S(2)}, u32[]{:S(2)}) %collective-permute-start.4) | collective-permute-done | bytes 524320 | tf_op jit(solution)/shard_map/ppermute | solution.py:33
  147.7 4.3 %attend.6.refs_0_ = bf16[16,128,128]{2,1,0:T(8,128)(2,1)S(1)} custom-call(s32[96]{0:T(128)S(1)} %reshape.29.list_ref, bf16[16,3,128,128]{3,2,1,0:T(8,128)(2,1)} %all-to-all-done.2.own, bf16[8,2,128,128]{3,2,1,0:T(8,128)(2,1)S(1)} %collective-permute-done.4.halo), custom_call_target="tpu_custom_call" | custom-call | flops 805306368 | bytes 2097152 | tf_op jit(solution)/shard_map/attend/pallas_call | solution.py:215
  152.0 3.4 %collective-permute-done.3.halo = bf16[8,2,128,128]{3,2,1,0:T(8,128)(2,1)S(1)} collective-permute-done((bf16[8,2,128,128]{3,2,1,0:T(8,128)(2,1)S(1)}, bf16[8,2,128,128]{3,2,1,0:T(8,128)(2,1)S(1)}, u32[]{:S(2)}, u32[]{:S(2)}) %collective-permute-start.3) | collective-permute-done | bytes 524320 | tf_op jit(solution)/shard_map/ppermute | solution.py:33
  155.4 4.3 %attend.7 = bf16[16,128,128]{2,1,0:T(8,128)(2,1)S(1)} custom-call(s32[96]{0:T(128)S(1)} %reshape.28.list_ref, bf16[16,3,128,128]{3,2,1,0:T(8,128)(2,1)} %all-to-all-done.2.own, bf16[8,2,128,128]{3,2,1,0:T(8,128)(2,1)S(1)} %collective-permute-done.3.halo, bf16[16,128,128]{2,1,0:T(8,128)(2,1)S(1)} %attend.6.refs_0_), custom_call_target="tpu_custom_call", output_to_operand_aliasing={{}: (3, {})} | custom-call | flops 805306368 | bytes 2097152 | tf_op jit(solution)/shard_map/attend/pallas_call | solution.py:215
  159.7 24.2 %all_to_all.20.refs_1_ = bf16[16,128,128]{2,1,0:T(8,128)(2,1)S(1)} all-to-all(bf16[16,128,128]{2,1,0:T(8,128)(2,1)S(1)} %attend.7), channel_id=1, replica_groups=mesh['blk'=16,'uly'=16] {'uly'}, dimensions={0} | all-to-all | bytes 1048576 | tf_op jit(solution)/shard_map/all_to_all | solution.py:47
  183.9 1.7 unpack.1
  (24 shorter events, 4.4 us)
Async XLA Ops:
  3.8 9.4 %copy-start.5 = (s32[3,16,12]{2,1,0:T(8,128)S(1)}, s32[3,16,12]{2,1,0:T(8,128)}, u32[]{:S(2)}) copy-start(s32[3,16,12]{2,1,0:T(8,128)} %param.8) | copy-start | bytes 6916
  3.8 9.4 %copy-start.6 = (s32[3,16,12]{2,1,0:T(8,128)S(1)}, s32[3,16,12]{2,1,0:T(8,128)}, u32[]{:S(2)}) copy-start(s32[3,16,12]{2,1,0:T(8,128)} %param.9) | copy-start | bytes 6916
  3.8 81.9 %all-to-all-start = ((bf16[16,3,128,256]{3,2,1,0:T(8,128)(2,1)}), bf16[16,3,128,256]{3,2,1,0:T(8,128)(2,1)S(1)}, u32[]{:S(2)}, u32[]{:S(2)}) async-start(bf16[16,3,128,256]{3,2,1,0:T(8,128)(2,1)} %pack.3), calls=%async_computation | async-start | bytes 6291456 | tf_op jit(solution)/shard_map/all_to_all | solution.py:47
  13.3 7.3 %collective-permute-start = (s32[3,16,12]{2,1,0:T(8,128)S(1)}, s32[3,16,12]{2,1,0:T(8,128)S(1)}, u32[]{:S(2)}, u32[]{:S(2)}) collective-permute-start(s32[3,16,12]{2,1,0:T(8,128)S(1)} %clamp_select_fusion), channel_id=1, source_target_pairs={{0,0},{1,1},{2,2},{3,3},{4,4},{5,5},{6,6},{7,7},{8,8},{9,9},{10,10... | collective-permute-start | bytes 6920 | tf_op jit(solution)/shard_map/ppermute | solution.py:43
  13.9 1.4 copy-start.1
  15.3 1.4 copy-start.2
  16.7 1.4 copy-start.3
  19.5 1.1 copy-start
  85.8 39.9 %all-to-all-start.2 = ((bf16[16,3,128,128]{3,2,1,0:T(8,128)(2,1)}), bf16[16,3,128,128]{3,2,1,0:T(8,128)(2,1)}, u32[]{:S(2)}, u32[]{:S(2)}) async-start(bf16[16,3,128,128]{3,2,1,0:T(8,128)(2,1)} %copy-done), calls=%async_computation.2 | async-start | bytes 3145728 | tf_op jit(solution)/shard_map/all_to_all | solution.py:47
  91.6 18.4 %collective-permute-start.2 = (bf16[8,2,128,256]{3,2,1,0:T(8,128)(2,1)}, bf16[8,2,128,256]{3,2,1,0:T(8,128)(2,1)}, u32[]{:S(2)}, u32[]{:S(2)}) collective-permute-start(bf16[8,2,128,256]{3,2,1,0:T(8,128)(2,1)} %get-tuple-element.11), channel_id=1, source_target_pairs={{0,16},{1,17},{2,18},{3,19},{4,20},{5,21},{6,22},{7,23},{8,24},{9,... | collective-permute-start | bytes 3145736 | tf_op jit(solution)/shard_map/ppermute | solution.py:33
  98.0 19.9 %collective-permute-start.1 = (bf16[8,2,128,256]{3,2,1,0:T(8,128)(2,1)}, bf16[8,2,128,256]{3,2,1,0:T(8,128)(2,1)}, u32[]{:S(2)}, u32[]{:S(2)}) collective-permute-start(bf16[8,2,128,256]{3,2,1,0:T(8,128)(2,1)} %get-tuple-element.12), channel_id=1, source_target_pairs={{16,0},{17,1},{18,2},{19,3},{20,4},{21,5},{22,6},{23,7},{24,8},{25... | collective-permute-start | bytes 3145736 | tf_op jit(solution)/shard_map/ppermute | solution.py:33
  124.6 1.0 copy-start.4
  125.6 34.1 %all-to-all-start.1 = ((bf16[16,128,256]{2,1,0:T(8,128)(2,1)}), bf16[16,128,256]{2,1,0:T(8,128)(2,1)S(1)}, u32[]{:S(2)}, u32[]{:S(2)}) async-start(bf16[16,128,256]{2,1,0:T(8,128)(2,1)} %copy-done.4), calls=%async_computation.1 | async-start | bytes 2097152 | tf_op jit(solution)/shard_map/all_to_all | solution.py:47
  134.3 13.3 %collective-permute-start.4 = (bf16[8,2,128,128]{3,2,1,0:T(8,128)(2,1)S(1)}, bf16[8,2,128,128]{3,2,1,0:T(8,128)(2,1)S(1)}, u32[]{:S(2)}, u32[]{:S(2)}) collective-permute-start(bf16[8,2,128,128]{3,2,1,0:T(8,128)(2,1)S(1)} %get-tuple-element.13), channel_id=1, source_target_pairs={{0,16},{1,17},{2,18},{3,19},{4,20},{5,21},{6,22},{7,23},{8,24},{9,... | collective-permute-start | bytes 1572872 | tf_op jit(solution)/shard_map/ppermute | solution.py:33
  141.6 13.8 %collective-permute-start.3 = (bf16[8,2,128,128]{3,2,1,0:T(8,128)(2,1)S(1)}, bf16[8,2,128,128]{3,2,1,0:T(8,128)(2,1)S(1)}, u32[]{:S(2)}, u32[]{:S(2)}) collective-permute-start(bf16[8,2,128,128]{3,2,1,0:T(8,128)(2,1)S(1)} %get-tuple-element.14), channel_id=1, source_target_pairs={{16,0},{17,1},{18,2},{19,3},{20,4},{21,5},{22,6},{23,7},{24,8},{25... | collective-permute-start | bytes 1572872 | tf_op jit(solution)/shard_map/ppermute | solution.py:33

commit v4 on v3

--- a/solution.py
+++ b/solution.py
@@ -12,9 +12,9 @@
 HEAD_DIM = 128
 HEAD_SETS = (2, 1)
 REACH = 8
-PACK_VMEM = 12 * 1024 * 1024
+PACK_VMEM = 8 * 1024 * 1024
 FIRST_PACK_VMEM = 63 * 1024 * 1024
-ATTEND_VMEM = 24 * 1024 * 1024
+ATTEND_VMEM = 10 * 1024 * 1024
 
 
 def flipped(slab, slabs):
@@ -92,27 +92,35 @@
     )(turn, *inputs)
 
 
-def unpack_kernel(widths, turn_ref, *refs):
-    inputs, out = refs[:-1], refs[-1]
-    per_group = sum(widths)
-    for group in range(out.shape[1] // per_group):
-        column = group * per_group
-        for ref, width in zip(inputs, widths):
-            out[:, column : column + width] = ref[group ^ turn_ref[0]]
-            column += width
+def unpack_kernel(widths, chunks, turn_ref, *refs):
+    inputs, (out, held, sems) = refs[: len(widths)], refs[len(widths) :]
+    groups, per_group = inputs[0].shape[0], sum(widths)
+    per_chunk = groups // chunks
+    copies = []
+    for chunk in range(chunks):
+        for group in range(chunk * per_chunk, (chunk + 1) * per_chunk):
+            column = group * per_group
+            for ref, width in zip(inputs, widths):
+                held[:, column : column + width] = ref[group ^ turn_ref[0]]
+                column += width
+        here = pl.ds(chunk * per_chunk * per_group, per_chunk * per_group)
+        copies.append(pltpu.make_async_copy(held.at[:, here], out.at[:, here], sems.at[chunk]))
+        copies[-1].start()
+    for copy in copies:
+        copy.wait()
 
 
 def unpack(parts, turn, groups):
     widths = [part.shape[-1] for part in parts]
-    per_step = 4
-    columns = per_step * sum(widths)
+    chunks = 4
+    shape = (TILE, groups * sum(widths))
     return pl.pallas_call(
-        functools.partial(unpack_kernel, widths),
-        grid=(groups // per_step,),
+        functools.partial(unpack_kernel, widths, chunks),
         in_specs=[pl.BlockSpec(memory_space=pltpu.SMEM)]
-        + [pl.BlockSpec((per_step, TILE, width), lambda g: (g, 0, 0)) for width in widths],
-        out_specs=pl.BlockSpec((TILE, columns), lambda g: (0, g)),
-        out_shape=jax.ShapeDtypeStruct((TILE, groups * sum(widths)), jnp.bfloat16),
+        + [pl.BlockSpec(memory_space=pltpu.VMEM)] * len(parts),
+        out_specs=pl.BlockSpec(memory_space=pl.ANY),
+        out_shape=jax.ShapeDtypeStruct(shape, jnp.bfloat16),
+        scratch_shapes=[pltpu.VMEM(shape, jnp.bfloat16), pltpu.SemaphoreType.DMA((chunks,))],
         compiler_params=pltpu.CompilerParams(vmem_limit_bytes=PACK_VMEM),
         name="unpack",
     )(turn, *parts)

time: 186 us -> 186 us (level)
  no operation moved by 1% of the time
where the time goes in v4:
time: 186 us; the launch traced here: 185 us
  waiting for transfers between devices  83.5 us (45%)
  starting transfers between devices  39.4 us (21%)
  Pallas kernels  28.3 us (15%)
  blocking collectives  24.2 us (13%)
  local copies, waits for them, and re-layouts  9.39 us (5%)
    all_to_all x3, waiting for transfers between devices, exchanged(): return lax.all_to_all(x, 'uly', split_axis=0, concat_axis=0, tiled=True)  65.2 us
    all_to_all x1, blocking collectives, exchanged(): return lax.all_to_all(x, 'uly', split_axis=0, concat_axis=0, tiled=True)  24.2 us
    pallas_call x4, Pallas kernels, attend(): pl.pallas_call(functools.partial(attend_kernel, first_tile, tiles, slots,...  22 us
    all_to_all x3, starting transfers between devices, exchanged(): return lax.all_to_all(x, 'uly', split_axis=0, concat_axis=0, tiled=True)  21.1 us
    ppermute x4, waiting for transfers between devices, to_neighbour(): return lax.ppermute(x, ('blk', 'uly'), pairs)  18.3 us
    ppermute x4, starting transfers between devices, to_neighbour(): return lax.ppermute(x, ('blk', 'uly'), pairs)  17.6 us
    unnamed x14, local copies, waits for them, and re-layouts  6.34 us
    pallas_call x2, Pallas kernels, pack(): pl.pallas_call(functools.partial(pack_kernel, columns // groups, skipped)...  5.1 us
  transfers between devices with their start and end apart: 8, of which 6 were waited for; matrix products, arithmetic and copies ran while one was open for 2% of the time, Pallas kernels for 13%

profile of v4, /device:TPU:7, one launch (start us, length us, event | category | flops | bytes accessed | tf_op | source)
XLA Modules:
  0.0 185.3 jit_solution(1052668475326688781)
XLA Ops:
  0.0 3.8 %pack.3 = bf16[16,3,128,256]{3,2,1,0:T(8,128)(2,1)} custom-call(s32[1]{0:T(128)} %bitcast.turn_ref, bf16[128,6144]{1,0:T(8,128)(2,1)} %refs_0_.3, bf16[128,6144]{1,0:T(8,128)(2,1)} %refs_1_.3, bf16[128,6144]{1,0:T(8,128)(2,1)} %refs_2_.3), custom_call_target="tpu_custom_call" | custom-call | bytes 7864320 | tf_op jit(solution)/shard_map/pack/pallas_call | solution.py:76
  3.8 9.3 %all-to-all-start = ((bf16[16,3,128,256]{3,2,1,0:T(8,128)(2,1)}), bf16[16,3,128,256]{3,2,1,0:T(8,128)(2,1)S(1)}, u32[]{:S(2)}, u32[]{:S(2)}) async-start(bf16[16,3,128,256]{3,2,1,0:T(8,128)(2,1)} %pack.3), calls=%async_computation | async-start | bytes 6291456 | tf_op jit(solution)/shard_map/all_to_all | solution.py:47
  13.9 1.4 copy-done.1
  15.3 1.4 copy-done.2
  16.7 1.4 copy-done.3
  18.2 1.3 pack.2
  20.6 65.1 %all-to-all-done.own = bf16[16,3,128,256]{3,2,1,0:T(8,128)(2,1)S(1)} async-done(((bf16[16,3,128,256]{3,2,1,0:T(8,128)(2,1)}), bf16[16,3,128,256]{3,2,1,0:T(8,128)(2,1)S(1)}, u32[]{:S(2)}, u32[]{:S(2)}) %all-to-all-start) | async-done | bytes 3145760 | tf_op jit(solution)/shard_map/all_to_all | solution.py:47
  85.8 4.4 %all-to-all-start.2 = ((bf16[16,3,128,128]{3,2,1,0:T(8,128)(2,1)}), bf16[16,3,128,128]{3,2,1,0:T(8,128)(2,1)}, u32[]{:S(2)}, u32[]{:S(2)}) async-start(bf16[16,3,128,128]{3,2,1,0:T(8,128)(2,1)} %copy-done), calls=%async_computation.2 | async-start | bytes 3145728 | tf_op jit(solution)/shard_map/all_to_all | solution.py:47
  90.2 1.4 fusion.1
  91.6 6.4 %collective-permute-start.2 = (bf16[8,2,128,256]{3,2,1,0:T(8,128)(2,1)}, bf16[8,2,128,256]{3,2,1,0:T(8,128)(2,1)}, u32[]{:S(2)}, u32[]{:S(2)}) collective-permute-start(bf16[8,2,128,256]{3,2,1,0:T(8,128)(2,1)} %get-tuple-element.11), channel_id=1, source_target_pairs={{0,16},{1,17},{2,18},{3,19},{4,20},{5,21},{6,22},{7,23},{8,24},{9,... | collective-permute-start | bytes 3145736 | tf_op jit(solution)/shard_map/ppermute | solution.py:33
  98.0 1.9 %collective-permute-start.1 = (bf16[8,2,128,256]{3,2,1,0:T(8,128)(2,1)}, bf16[8,2,128,256]{3,2,1,0:T(8,128)(2,1)}, u32[]{:S(2)}, u32[]{:S(2)}) collective-permute-start(bf16[8,2,128,256]{3,2,1,0:T(8,128)(2,1)} %get-tuple-element.12), channel_id=1, source_target_pairs={{16,0},{17,1},{18,2},{19,3},{20,4},{21,5},{22,6},{23,7},{24,8},{25... | collective-permute-start | bytes 3145736 | tf_op jit(solution)/shard_map/ppermute | solution.py:33
  100.1 9.9 %collective-permute-done.2.halo = bf16[8,2,128,256]{3,2,1,0:T(8,128)(2,1)} collective-permute-done((bf16[8,2,128,256]{3,2,1,0:T(8,128)(2,1)}, bf16[8,2,128,256]{3,2,1,0:T(8,128)(2,1)}, u32[]{:S(2)}, u32[]{:S(2)}) %collective-permute-start.2) | collective-permute-done | bytes 1048608 | tf_op jit(solution)/shard_map/ppermute | solution.py:33
  110.0 6.7 %attend.4.refs_0_ = bf16[16,128,256]{2,1,0:T(8,128)(2,1)S(1)} custom-call(s32[192]{0:T(256)S(1)} %reshape.27.list_ref, bf16[16,3,128,256]{3,2,1,0:T(8,128)(2,1)S(1)} %all-to-all-done.own, bf16[8,2,128,256]{3,2,1,0:T(8,128)(2,1)} %collective-permute-done.2.halo), custom_call_target="tpu_custom_call" | custom-call | flops 1610612736 | bytes 4194304 | tf_op jit(solution)/shard_map/attend/pallas_call | solution.py:223
  117.9 6.7 %attend.5 = bf16[16,128,256]{2,1,0:T(8,128)(2,1)S(1)} custom-call(s32[192]{0:T(256)S(1)} %reshape.26.list_ref, bf16[16,3,128,256]{3,2,1,0:T(8,128)(2,1)S(1)} %all-to-all-done.own, bf16[8,2,128,256]{3,2,1,0:T(8,128)(2,1)} %collective-permute-done.1.halo, bf16[16,128,256]{2,1,0:T(8,128)(2,1)S(1)} %attend.4.refs_0_), custom_call_target="tpu_custom_call", output_to_operand_aliasing={{}: (3, {})} | custom-call | flops 1610612736 | bytes 4194304 | tf_op jit(solution)/shard_map/attend/pallas_call | solution.py:223
  125.6 7.4 %all-to-all-start.1 = ((bf16[16,128,256]{2,1,0:T(8,128)(2,1)}), bf16[16,128,256]{2,1,0:T(8,128)(2,1)S(1)}, u32[]{:S(2)}, u32[]{:S(2)}) async-start(bf16[16,128,256]{2,1,0:T(8,128)(2,1)} %copy-done.4), calls=%async_computation.1 | async-start | bytes 2097152 | tf_op jit(solution)/shard_map/all_to_all | solution.py:47
  133.1 1.3 fusion.2
  134.3 7.2 %collective-permute-start.4 = (bf16[8,2,128,128]{3,2,1,0:T(8,128)(2,1)S(1)}, bf16[8,2,128,128]{3,2,1,0:T(8,128)(2,1)S(1)}, u32[]{:S(2)}, u32[]{:S(2)}) collective-permute-start(bf16[8,2,128,128]{3,2,1,0:T(8,128)(2,1)S(1)} %get-tuple-element.13), channel_id=1, source_target_pairs={{0,16},{1,17},{2,18},{3,19},{4,20},{5,21},{6,22},{7,23},{8,24},{9,... | collective-permute-start | bytes 1572872 | tf_op jit(solution)/shard_map/ppermute | solution.py:33
  141.6 2.1 %collective-permute-start.3 = (bf16[8,2,128,128]{3,2,1,0:T(8,128)(2,1)S(1)}, bf16[8,2,128,128]{3,2,1,0:T(8,128)(2,1)S(1)}, u32[]{:S(2)}, u32[]{:S(2)}) collective-permute-start(bf16[8,2,128,128]{3,2,1,0:T(8,128)(2,1)S(1)} %get-tuple-element.14), channel_id=1, source_target_pairs={{16,0},{17,1},{18,2},{19,3},{20,4},{21,5},{22,6},{23,7},{24,8},{25... | collective-permute-start | bytes 1572872 | tf_op jit(solution)/shard_map/ppermute | solution.py:33
  143.9 3.8 %collective-permute-done.4.halo = bf16[8,2,128,128]{3,2,1,0:T(8,128)(2,1)S(1)} collective-permute-done((bf16[8,2,128,128]{3,2,1,0:T(8,128)(2,1)S(1)}, bf16[8,2,128,128]{3,2,1,0:T(8,128)(2,1)S(1)}, u32[]{:S(2)}, u32[]{:S(2)}) %collective-permute-start.4) | collective-permute-done | bytes 524320 | tf_op jit(solution)/shard_map/ppermute | solution.py:33
  147.7 4.3 %attend.6.refs_0_ = bf16[16,128,128]{2,1,0:T(8,128)(2,1)S(1)} custom-call(s32[96]{0:T(128)S(1)} %reshape.29.list_ref, bf16[16,3,128,128]{3,2,1,0:T(8,128)(2,1)} %all-to-all-done.2.own, bf16[8,2,128,128]{3,2,1,0:T(8,128)(2,1)S(1)} %collective-permute-done.4.halo), custom_call_target="tpu_custom_call" | custom-call | flops 805306368 | bytes 2097152 | tf_op jit(solution)/shard_map/attend/pallas_call | solution.py:223
  152.0 3.4 %collective-permute-done.3.halo = bf16[8,2,128,128]{3,2,1,0:T(8,128)(2,1)S(1)} collective-permute-done((bf16[8,2,128,128]{3,2,1,0:T(8,128)(2,1)S(1)}, bf16[8,2,128,128]{3,2,1,0:T(8,128)(2,1)S(1)}, u32[]{:S(2)}, u32[]{:S(2)}) %collective-permute-start.3) | collective-permute-done | bytes 524320 | tf_op jit(solution)/shard_map/ppermute | solution.py:33
  155.4 4.3 %attend.7 = bf16[16,128,128]{2,1,0:T(8,128)(2,1)S(1)} custom-call(s32[96]{0:T(128)S(1)} %reshape.28.list_ref, bf16[16,3,128,128]{3,2,1,0:T(8,128)(2,1)} %all-to-all-done.2.own, bf16[8,2,128,128]{3,2,1,0:T(8,128)(2,1)S(1)} %collective-permute-done.3.halo, bf16[16,128,128]{2,1,0:T(8,128)(2,1)S(1)} %attend.6.refs_0_), custom_call_target="tpu_custom_call", output_to_operand_aliasing={{}: (3, {})} | custom-call | flops 805306368 | bytes 2097152 | tf_op jit(solution)/shard_map/attend/pallas_call | solution.py:223
  159.7 24.2 %all_to_all.20.refs_1_ = bf16[16,128,128]{2,1,0:T(8,128)(2,1)S(1)} all-to-all(bf16[16,128,128]{2,1,0:T(8,128)(2,1)S(1)} %attend.7), channel_id=1, replica_groups=mesh['blk'=16,'uly'=16] {'uly'}, dimensions={0} | all-to-all | bytes 1048576 | tf_op jit(solution)/shard_map/all_to_all | solution.py:47
  183.9 1.2 unpack.1
  (24 shorter events, 4.4 us)
Async XLA Ops:
  3.8 9.4 %copy-start.5 = (s32[3,16,12]{2,1,0:T(8,128)S(1)}, s32[3,16,12]{2,1,0:T(8,128)}, u32[]{:S(2)}) copy-start(s32[3,16,12]{2,1,0:T(8,128)} %param.8) | copy-start | bytes 6916
  3.8 9.4 %copy-start.6 = (s32[3,16,12]{2,1,0:T(8,128)S(1)}, s32[3,16,12]{2,1,0:T(8,128)}, u32[]{:S(2)}) copy-start(s32[3,16,12]{2,1,0:T(8,128)} %param.9) | copy-start | bytes 6916
  3.8 81.9 %all-to-all-start = ((bf16[16,3,128,256]{3,2,1,0:T(8,128)(2,1)}), bf16[16,3,128,256]{3,2,1,0:T(8,128)(2,1)S(1)}, u32[]{:S(2)}, u32[]{:S(2)}) async-start(bf16[16,3,128,256]{3,2,1,0:T(8,128)(2,1)} %pack.3), calls=%async_computation | async-start | bytes 6291456 | tf_op jit(solution)/shard_map/all_to_all | solution.py:47
  13.3 7.3 %collective-permute-start = (s32[3,16,12]{2,1,0:T(8,128)S(1)}, s32[3,16,12]{2,1,0:T(8,128)S(1)}, u32[]{:S(2)}, u32[]{:S(2)}) collective-permute-start(s32[3,16,12]{2,1,0:T(8,128)S(1)} %clamp_select_fusion), channel_id=1, source_target_pairs={{0,0},{1,1},{2,2},{3,3},{4,4},{5,5},{6,6},{7,7},{8,8},{9,9},{10,10... | collective-permute-start | bytes 6920 | tf_op jit(solution)/shard_map/ppermute | solution.py:43
  13.9 1.4 copy-start.1
  15.3 1.4 copy-start.2
  16.7 1.4 copy-start.3
  19.5 1.1 copy-start
  85.8 39.9 %all-to-all-start.2 = ((bf16[16,3,128,128]{3,2,1,0:T(8,128)(2,1)}), bf16[16,3,128,128]{3,2,1,0:T(8,128)(2,1)}, u32[]{:S(2)}, u32[]{:S(2)}) async-start(bf16[16,3,128,128]{3,2,1,0:T(8,128)(2,1)} %copy-done), calls=%async_computation.2 | async-start | bytes 3145728 | tf_op jit(solution)/shard_map/all_to_all | solution.py:47
  91.6 18.4 %collective-permute-start.2 = (bf16[8,2,128,256]{3,2,1,0:T(8,128)(2,1)}, bf16[8,2,128,256]{3,2,1,0:T(8,128)(2,1)}, u32[]{:S(2)}, u32[]{:S(2)}) collective-permute-start(bf16[8,2,128,256]{3,2,1,0:T(8,128)(2,1)} %get-tuple-element.11), channel_id=1, source_target_pairs={{0,16},{1,17},{2,18},{3,19},{4,20},{5,21},{6,22},{7,23},{8,24},{9,... | collective-permute-start | bytes 3145736 | tf_op jit(solution)/shard_map/ppermute | solution.py:33
  98.0 19.9 %collective-permute-start.1 = (bf16[8,2,128,256]{3,2,1,0:T(8,128)(2,1)}, bf16[8,2,128,256]{3,2,1,0:T(8,128)(2,1)}, u32[]{:S(2)}, u32[]{:S(2)}) collective-permute-start(bf16[8,2,128,256]{3,2,1,0:T(8,128)(2,1)} %get-tuple-element.12), channel_id=1, source_target_pairs={{16,0},{17,1},{18,2},{19,3},{20,4},{21,5},{22,6},{23,7},{24,8},{25... | collective-permute-start | bytes 3145736 | tf_op jit(solution)/shard_map/ppermute | solution.py:33
  124.6 1.0 copy-start.4
  125.6 34.1 %all-to-all-start.1 = ((bf16[16,128,256]{2,1,0:T(8,128)(2,1)}), bf16[16,128,256]{2,1,0:T(8,128)(2,1)S(1)}, u32[]{:S(2)}, u32[]{:S(2)}) async-start(bf16[16,128,256]{2,1,0:T(8,128)(2,1)} %copy-done.4), calls=%async_computation.1 | async-start | bytes 2097152 | tf_op jit(solution)/shard_map/all_to_all | solution.py:47
  134.3 13.3 %collective-permute-start.4 = (bf16[8,2,128,128]{3,2,1,0:T(8,128)(2,1)S(1)}, bf16[8,2,128,128]{3,2,1,0:T(8,128)(2,1)S(1)}, u32[]{:S(2)}, u32[]{:S(2)}) collective-permute-start(bf16[8,2,128,128]{3,2,1,0:T(8,128)(2,1)S(1)} %get-tuple-element.13), channel_id=1, source_target_pairs={{0,16},{1,17},{2,18},{3,19},{4,20},{5,21},{6,22},{7,23},{8,24},{9,... | collective-permute-start | bytes 1572872 | tf_op jit(solution)/shard_map/ppermute | solution.py:33
  141.6 13.8 %collective-permute-start.3 = (bf16[8,2,128,128]{3,2,1,0:T(8,128)(2,1)S(1)}, bf16[8,2,128,128]{3,2,1,0:T(8,128)(2,1)S(1)}, u32[]{:S(2)}, u32[]{:S(2)}) collective-permute-start(bf16[8,2,128,128]{3,2,1,0:T(8,128)(2,1)S(1)} %get-tuple-element.14), channel_id=1, source_target_pairs={{16,0},{17,1},{18,2},{19,3},{20,4},{21,5},{22,6},{23,7},{24,8},{25... | collective-permute-start | bytes 1572872 | tf_op jit(solution)/shard_map/ppermute | solution.py:33

commit v5 on v4

--- a/solution.py
+++ b/solution.py
@@ -14,7 +14,7 @@
 REACH = 8
 PACK_VMEM = 8 * 1024 * 1024
 FIRST_PACK_VMEM = 63 * 1024 * 1024
-ATTEND_VMEM = 10 * 1024 * 1024
+ATTEND_VMEM = 20 * 1024 * 1024
 
 
 def flipped(slab, slabs):
@@ -223,7 +223,8 @@
     return pl.pallas_call(
         functools.partial(attend_kernel, first_tile, tiles, slots, len(filled)),
         in_specs=[pl.BlockSpec(memory_space=pltpu.SMEM)]
-        + [pl.BlockSpec(memory_space=pl.ANY)] * (2 + len(filled)),
+        + [pl.BlockSpec(memory_space=pltpu.VMEM)] * 2
+        + [pl.BlockSpec(memory_space=pl.ANY)] * len(filled),
         out_specs=pl.BlockSpec(memory_space=pl.ANY),
         out_shape=jax.ShapeDtypeStruct((slab_tiles, TILE, width), jnp.bfloat16),
         scratch_shapes=[

time: 186 us -> 186 us (level)
  transfers between devices with their start and end apart: 8 -> 8, of which waited for: 6 -> 6; matrix products, arithmetic and copies ran while one was open for 2% -> 2% of each run, Pallas kernels for 13% -> 12%
where the time goes in v5:
time: 186 us; the launch traced here: 184 us
  waiting for transfers between devices  84.5 us (45%)
  starting transfers between devices  38.8 us (21%)
  Pallas kernels  27.2 us (15%)
  blocking collectives  23.4 us (13%)
  local copies, waits for them, and re-layouts  9.39 us (5%)
    all_to_all x3, waiting for transfers between devices, exchanged(): return lax.all_to_all(x, 'uly', split_axis=0, concat_axis=0, tiled=True)  65.5 us
    all_to_all x1, blocking collectives, exchanged(): return lax.all_to_all(x, 'uly', split_axis=0, concat_axis=0, tiled=True)  23.4 us
    all_to_all x3, starting transfers between devices, exchanged(): return lax.all_to_all(x, 'uly', split_axis=0, concat_axis=0, tiled=True)  21.1 us
    pallas_call x4, Pallas kernels, attend(): pl.pallas_call(functools.partial(attend_kernel, first_tile, tiles, slots,...  20.9 us
    ppermute x4, waiting for transfers between devices, to_neighbour(): return lax.ppermute(x, ('blk', 'uly'), pairs)  19 us
    ppermute x4, starting transfers between devices, to_neighbour(): return lax.ppermute(x, ('blk', 'uly'), pairs)  17 us
    unnamed x14, local copies, waits for them, and re-layouts  6.34 us
    pallas_call x2, Pallas kernels, pack(): pl.pallas_call(functools.partial(pack_kernel, columns // groups, skipped)...  5.1 us
  transfers between devices with their start and end apart: 8, of which 6 were waited for; matrix products, arithmetic and copies ran while one was open for 2% of the time, Pallas kernels for 12%

profile of v5, /device:TPU:7, one launch (start us, length us, event | category | flops | bytes accessed | tf_op | source)
XLA Modules:
  0.0 183.8 jit_solution(17982776744828401853)
XLA Ops:
  0.0 3.8 %pack.3 = bf16[16,3,128,256]{3,2,1,0:T(8,128)(2,1)} custom-call(s32[1]{0:T(128)} %bitcast.turn_ref, bf16[128,6144]{1,0:T(8,128)(2,1)} %refs_0_.3, bf16[128,6144]{1,0:T(8,128)(2,1)} %refs_1_.3, bf16[128,6144]{1,0:T(8,128)(2,1)} %refs_2_.3), custom_call_target="tpu_custom_call" | custom-call | bytes 7864320 | tf_op jit(solution)/shard_map/pack/pallas_call | solution.py:76
  3.8 9.3 %all-to-all-start = ((bf16[16,3,128,256]{3,2,1,0:T(8,128)(2,1)}), bf16[16,3,128,256]{3,2,1,0:T(8,128)(2,1)S(1)}, u32[]{:S(2)}, u32[]{:S(2)}) async-start(bf16[16,3,128,256]{3,2,1,0:T(8,128)(2,1)} %pack.3), calls=%async_computation | async-start | bytes 6291456 | tf_op jit(solution)/shard_map/all_to_all | solution.py:47
  13.9 1.4 copy-done.1
  15.3 1.4 copy-done.2
  16.7 1.4 copy-done.3
  18.2 1.3 pack.2
  20.6 65.1 %all-to-all-done.own = bf16[16,3,128,256]{3,2,1,0:T(8,128)(2,1)S(1)} async-done(((bf16[16,3,128,256]{3,2,1,0:T(8,128)(2,1)}), bf16[16,3,128,256]{3,2,1,0:T(8,128)(2,1)S(1)}, u32[]{:S(2)}, u32[]{:S(2)}) %all-to-all-start) | async-done | bytes 3145760 | tf_op jit(solution)/shard_map/all_to_all | solution.py:47
  85.8 4.4 %all-to-all-start.2 = ((bf16[16,3,128,128]{3,2,1,0:T(8,128)(2,1)}), bf16[16,3,128,128]{3,2,1,0:T(8,128)(2,1)}, u32[]{:S(2)}, u32[]{:S(2)}) async-start(bf16[16,3,128,128]{3,2,1,0:T(8,128)(2,1)} %copy-done), calls=%async_computation.2 | async-start | bytes 3145728 | tf_op jit(solution)/shard_map/all_to_all | solution.py:47
  90.2 1.4 fusion.1
  91.6 6.4 %collective-permute-start.2 = (bf16[8,2,128,256]{3,2,1,0:T(8,128)(2,1)}, bf16[8,2,128,256]{3,2,1,0:T(8,128)(2,1)}, u32[]{:S(2)}, u32[]{:S(2)}) collective-permute-start(bf16[8,2,128,256]{3,2,1,0:T(8,128)(2,1)} %get-tuple-element.11), channel_id=1, source_target_pairs={{0,16},{1,17},{2,18},{3,19},{4,20},{5,21},{6,22},{7,23},{8,24},{9,... | collective-permute-start | bytes 3145736 | tf_op jit(solution)/shard_map/ppermute | solution.py:33
  98.0 1.9 %collective-permute-start.1 = (bf16[8,2,128,256]{3,2,1,0:T(8,128)(2,1)}, bf16[8,2,128,256]{3,2,1,0:T(8,128)(2,1)}, u32[]{:S(2)}, u32[]{:S(2)}) collective-permute-start(bf16[8,2,128,256]{3,2,1,0:T(8,128)(2,1)} %get-tuple-element.12), channel_id=1, source_target_pairs={{16,0},{17,1},{18,2},{19,3},{20,4},{21,5},{22,6},{23,7},{24,8},{25... | collective-permute-start | bytes 3145736 | tf_op jit(solution)/shard_map/ppermute | solution.py:33
  100.1 9.9 %collective-permute-done.2.halo = bf16[8,2,128,256]{3,2,1,0:T(8,128)(2,1)} collective-permute-done((bf16[8,2,128,256]{3,2,1,0:T(8,128)(2,1)}, bf16[8,2,128,256]{3,2,1,0:T(8,128)(2,1)}, u32[]{:S(2)}, u32[]{:S(2)}) %collective-permute-start.2) | collective-permute-done | bytes 1048608 | tf_op jit(solution)/shard_map/ppermute | solution.py:33
  110.0 6.4 %attend.4.refs_0_ = bf16[16,128,256]{2,1,0:T(8,128)(2,1)S(1)} custom-call(s32[192]{0:T(256)S(1)} %reshape.27.list_ref, bf16[16,3,128,256]{3,2,1,0:T(8,128)(2,1)S(1)} %all-to-all-done.own, bf16[8,2,128,256]{3,2,1,0:T(8,128)(2,1)} %collective-permute-done.2.halo), custom_call_target="tpu_custom_call" | custom-call | flops 1610612736 | bytes 4194304 | tf_op jit(solution)/shard_map/attend/pallas_call | solution.py:223
  116.4 1.4 collective-permute-done.1.halo
  117.9 6.4 %attend.5 = bf16[16,128,256]{2,1,0:T(8,128)(2,1)S(1)} custom-call(s32[192]{0:T(256)S(1)} %reshape.26.list_ref, bf16[16,3,128,256]{3,2,1,0:T(8,128)(2,1)S(1)} %all-to-all-done.own, bf16[8,2,128,256]{3,2,1,0:T(8,128)(2,1)} %collective-permute-done.1.halo, bf16[16,128,256]{2,1,0:T(8,128)(2,1)S(1)} %attend.4.refs_0_), custom_call_target="tpu_custom_call", output_to_operand_aliasing={{}: (3, {})} | custom-call | flops 1610612736 | bytes 4194304 | tf_op jit(solution)/shard_map/attend/pallas_call | solution.py:223
  125.6 7.4 %all-to-all-start.1 = ((bf16[16,128,256]{2,1,0:T(8,128)(2,1)}), bf16[16,128,256]{2,1,0:T(8,128)(2,1)S(1)}, u32[]{:S(2)}, u32[]{:S(2)}) async-start(bf16[16,128,256]{2,1,0:T(8,128)(2,1)} %copy-done.4), calls=%async_computation.1 | async-start | bytes 2097152 | tf_op jit(solution)/shard_map/all_to_all | solution.py:47
  133.1 1.3 fusion.2
  134.3 6.7 %collective-permute-start.4 = (bf16[8,2,128,128]{3,2,1,0:T(8,128)(2,1)S(1)}, bf16[8,2,128,128]{3,2,1,0:T(8,128)(2,1)S(1)}, u32[]{:S(2)}, u32[]{:S(2)}) collective-permute-start(bf16[8,2,128,128]{3,2,1,0:T(8,128)(2,1)S(1)} %get-tuple-element.13), channel_id=1, source_target_pairs={{0,16},{1,17},{2,18},{3,19},{4,20},{5,21},{6,22},{7,23},{8,24},{9,... | collective-permute-start | bytes 1572872 | tf_op jit(solution)/shard_map/ppermute | solution.py:33
  141.0 2.1 %collective-permute-start.3 = (bf16[8,2,128,128]{3,2,1,0:T(8,128)(2,1)S(1)}, bf16[8,2,128,128]{3,2,1,0:T(8,128)(2,1)S(1)}, u32[]{:S(2)}, u32[]{:S(2)}) collective-permute-start(bf16[8,2,128,128]{3,2,1,0:T(8,128)(2,1)S(1)} %get-tuple-element.14), channel_id=1, source_target_pairs={{16,0},{17,1},{18,2},{19,3},{20,4},{21,5},{22,6},{23,7},{24,8},{25... | collective-permute-start | bytes 1572872 | tf_op jit(solution)/shard_map/ppermute | solution.py:33
  143.3 3.8 %collective-permute-done.4.halo = bf16[8,2,128,128]{3,2,1,0:T(8,128)(2,1)S(1)} collective-permute-done((bf16[8,2,128,128]{3,2,1,0:T(8,128)(2,1)S(1)}, bf16[8,2,128,128]{3,2,1,0:T(8,128)(2,1)S(1)}, u32[]{:S(2)}, u32[]{:S(2)}) %collective-permute-start.4) | collective-permute-done | bytes 524320 | tf_op jit(solution)/shard_map/ppermute | solution.py:33
  147.1 4.0 %attend.6.refs_0_ = bf16[16,128,128]{2,1,0:T(8,128)(2,1)S(1)} custom-call(s32[96]{0:T(128)S(1)} %reshape.29.list_ref, bf16[16,3,128,128]{3,2,1,0:T(8,128)(2,1)} %all-to-all-done.2.own, bf16[8,2,128,128]{3,2,1,0:T(8,128)(2,1)S(1)} %collective-permute-done.4.halo), custom_call_target="tpu_custom_call" | custom-call | flops 805306368 | bytes 2097152 | tf_op jit(solution)/shard_map/attend/pallas_call | solution.py:223
  151.2 3.8 %collective-permute-done.3.halo = bf16[8,2,128,128]{3,2,1,0:T(8,128)(2,1)S(1)} collective-permute-done((bf16[8,2,128,128]{3,2,1,0:T(8,128)(2,1)S(1)}, bf16[8,2,128,128]{3,2,1,0:T(8,128)(2,1)S(1)}, u32[]{:S(2)}, u32[]{:S(2)}) %collective-permute-start.3) | collective-permute-done | bytes 524320 | tf_op jit(solution)/shard_map/ppermute | solution.py:33
  155.0 4.0 %attend.7 = bf16[16,128,128]{2,1,0:T(8,128)(2,1)S(1)} custom-call(s32[96]{0:T(128)S(1)} %reshape.28.list_ref, bf16[16,3,128,128]{3,2,1,0:T(8,128)(2,1)} %all-to-all-done.2.own, bf16[8,2,128,128]{3,2,1,0:T(8,128)(2,1)S(1)} %collective-permute-done.3.halo, bf16[16,128,128]{2,1,0:T(8,128)(2,1)S(1)} %attend.6.refs_0_), custom_call_target="tpu_custom_call", output_to_operand_aliasing={{}: (3, {})} | custom-call | flops 805306368 | bytes 2097152 | tf_op jit(solution)/shard_map/attend/pallas_call | solution.py:223
  159.0 23.4 %all_to_all.20.refs_1_ = bf16[16,128,128]{2,1,0:T(8,128)(2,1)S(1)} all-to-all(bf16[16,128,128]{2,1,0:T(8,128)(2,1)S(1)} %attend.7), channel_id=1, replica_groups=mesh['blk'=16,'uly'=16] {'uly'}, dimensions={0} | all-to-all | bytes 1048576 | tf_op jit(solution)/shard_map/all_to_all | solution.py:47
  (24 shorter events, 4.8 us)
Async XLA Ops:
  3.8 9.4 %copy-start.5 = (s32[3,16,12]{2,1,0:T(8,128)S(1)}, s32[3,16,12]{2,1,0:T(8,128)}, u32[]{:S(2)}) copy-start(s32[3,16,12]{2,1,0:T(8,128)} %param.8) | copy-start | bytes 6916
  3.8 9.4 %copy-start.6 = (s32[3,16,12]{2,1,0:T(8,128)S(1)}, s32[3,16,12]{2,1,0:T(8,128)}, u32[]{:S(2)}) copy-start(s32[3,16,12]{2,1,0:T(8,128)} %param.9) | copy-start | bytes 6916
  3.8 81.9 %all-to-all-start = ((bf16[16,3,128,256]{3,2,1,0:T(8,128)(2,1)}), bf16[16,3,128,256]{3,2,1,0:T(8,128)(2,1)S(1)}, u32[]{:S(2)}, u32[]{:S(2)}) async-start(bf16[16,3,128,256]{3,2,1,0:T(8,128)(2,1)} %pack.3), calls=%async_computation | async-start | bytes 6291456 | tf_op jit(solution)/shard_map/all_to_all | solution.py:47
  13.3 7.3 %collective-permute-start = (s32[3,16,12]{2,1,0:T(8,128)S(1)}, s32[3,16,12]{2,1,0:T(8,128)S(1)}, u32[]{:S(2)}, u32[]{:S(2)}) collective-permute-start(s32[3,16,12]{2,1,0:T(8,128)S(1)} %clamp_select_fusion), channel_id=1, source_target_pairs={{0,0},{1,1},{2,2},{3,3},{4,4},{5,5},{6,6},{7,7},{8,8},{9,9},{10,10... | collective-permute-start | bytes 6920 | tf_op jit(solution)/shard_map/ppermute | solution.py:43
  13.9 1.4 copy-start.1
  15.3 1.4 copy-start.2
  16.7 1.4 copy-start.3
  19.5 1.1 copy-start
  85.8 39.9 %all-to-all-start.2 = ((bf16[16,3,128,128]{3,2,1,0:T(8,128)(2,1)}), bf16[16,3,128,128]{3,2,1,0:T(8,128)(2,1)}, u32[]{:S(2)}, u32[]{:S(2)}) async-start(bf16[16,3,128,128]{3,2,1,0:T(8,128)(2,1)} %copy-done), calls=%async_computation.2 | async-start | bytes 3145728 | tf_op jit(solution)/shard_map/all_to_all | solution.py:47
  91.6 18.4 %collective-permute-start.2 = (bf16[8,2,128,256]{3,2,1,0:T(8,128)(2,1)}, bf16[8,2,128,256]{3,2,1,0:T(8,128)(2,1)}, u32[]{:S(2)}, u32[]{:S(2)}) collective-permute-start(bf16[8,2,128,256]{3,2,1,0:T(8,128)(2,1)} %get-tuple-element.11), channel_id=1, source_target_pairs={{0,16},{1,17},{2,18},{3,19},{4,20},{5,21},{6,22},{7,23},{8,24},{9,... | collective-permute-start | bytes 3145736 | tf_op jit(solution)/shard_map/ppermute | solution.py:33
  98.0 19.9 %collective-permute-start.1 = (bf16[8,2,128,256]{3,2,1,0:T(8,128)(2,1)}, bf16[8,2,128,256]{3,2,1,0:T(8,128)(2,1)}, u32[]{:S(2)}, u32[]{:S(2)}) collective-permute-start(bf16[8,2,128,256]{3,2,1,0:T(8,128)(2,1)} %get-tuple-element.12), channel_id=1, source_target_pairs={{16,0},{17,1},{18,2},{19,3},{20,4},{21,5},{22,6},{23,7},{24,8},{25... | collective-permute-start | bytes 3145736 | tf_op jit(solution)/shard_map/ppermute | solution.py:33
  124.3 1.0 copy-start.4
  125.6 33.4 %all-to-all-start.1 = ((bf16[16,128,256]{2,1,0:T(8,128)(2,1)}), bf16[16,128,256]{2,1,0:T(8,128)(2,1)S(1)}, u32[]{:S(2)}, u32[]{:S(2)}) async-start(bf16[16,128,256]{2,1,0:T(8,128)(2,1)} %copy-done.4), calls=%async_computation.1 | async-start | bytes 2097152 | tf_op jit(solution)/shard_map/all_to_all | solution.py:47
  134.3 12.8 %collective-permute-start.4 = (bf16[8,2,128,128]{3,2,1,0:T(8,128)(2,1)S(1)}, bf16[8,2,128,128]{3,2,1,0:T(8,128)(2,1)S(1)}, u32[]{:S(2)}, u32[]{:S(2)}) collective-permute-start(bf16[8,2,128,128]{3,2,1,0:T(8,128)(2,1)S(1)} %get-tuple-element.13), channel_id=1, source_target_pairs={{0,16},{1,17},{2,18},{3,19},{4,20},{5,21},{6,22},{7,23},{8,24},{9,... | collective-permute-start | bytes 1572872 | tf_op jit(solution)/shard_map/ppermute | solution.py:33
  141.0 14.0 %collective-permute-start.3 = (bf16[8,2,128,128]{3,2,1,0:T(8,128)(2,1)S(1)}, bf16[8,2,128,128]{3,2,1,0:T(8,128)(2,1)S(1)}, u32[]{:S(2)}, u32[]{:S(2)}) collective-permute-start(bf16[8,2,128,128]{3,2,1,0:T(8,128)(2,1)S(1)} %get-tuple-element.14), channel_id=1, source_target_pairs={{16,0},{17,1},{18,2},{19,3},{20,4},{21,5},{22,6},{23,7},{24,8},{25... | collective-permute-start | bytes 1572872 | tf_op jit(solution)/shard_map/ppermute | solution.py:33

commit v6 on v5

--- a/solution.py
+++ b/solution.py
@@ -148,7 +148,7 @@
     value[window_tiles] = jnp.zeros((TILE, width), jnp.bfloat16)
     counted[0] = jnp.zeros((TILE, HEAD_DIM), jnp.bfloat16)
     counted[1] = jnp.ones((TILE, HEAD_DIM), jnp.bfloat16)
-    for copy in copies:
+    for copy in (copies[0], copies[1], copies[3]):
         copy.wait()
     factor = math.log2(math.e) / math.sqrt(HEAD_DIM)
 
@@ -197,6 +197,8 @@
     together = tiles
     steps = [(tile, head) for tile in range(together) for head in range(heads)]
     score(0, 0, 0)
+    for copy in (copies[2], copies[4]):
+        copy.wait()
 
     def some_tiles(n, carry):
         first = n * together

time: 186 us -> 186 us (level)
  no operation moved by 1% of the time
where the time goes in v6:
time: 186 us; the launch traced here: 185 us
  waiting for transfers between devices  83.9 us (45%)
  starting transfers between devices  39.1 us (21%)
  Pallas kernels  27.8 us (15%)
  blocking collectives  24.4 us (13%)
  local copies, waits for them, and re-layouts  9.39 us (5%)
    all_to_all x3, waiting for transfers between devices, exchanged(): return lax.all_to_all(x, 'uly', split_axis=0, concat_axis=0, tiled=True)  65.4 us
    all_to_all x1, blocking collectives, exchanged(): return lax.all_to_all(x, 'uly', split_axis=0, concat_axis=0, tiled=True)  24.4 us
    pallas_call x4, Pallas kernels, attend(): pl.pallas_call(functools.partial(attend_kernel, first_tile, tiles, slots,...  21.5 us
    all_to_all x3, starting transfers between devices, exchanged(): return lax.all_to_all(x, 'uly', split_axis=0, concat_axis=0, tiled=True)  21.1 us
    ppermute x4, waiting for transfers between devices, to_neighbour(): return lax.ppermute(x, ('blk', 'uly'), pairs)  18.6 us
    ppermute x4, starting transfers between devices, to_neighbour(): return lax.ppermute(x, ('blk', 'uly'), pairs)  17.3 us
    unnamed x14, local copies, waits for them, and re-layouts  6.34 us
    pallas_call x2, Pallas kernels, pack(): pl.pallas_call(functools.partial(pack_kernel, columns // groups, skipped)...  5.1 us
  transfers between devices with their start and end apart: 8, of which 6 were waited for; matrix products, arithmetic and copies ran while one was open for 2% of the time, Pallas kernels for 12%

profile of v6, /device:TPU:7, one launch (start us, length us, event | category | flops | bytes accessed | tf_op | source)
XLA Modules:
  0.0 185.1 jit_solution(13130239147458964541)
XLA Ops:
  0.0 3.8 %pack.3 = bf16[16,3,128,256]{3,2,1,0:T(8,128)(2,1)} custom-call(s32[1]{0:T(128)} %bitcast.turn_ref, bf16[128,6144]{1,0:T(8,128)(2,1)} %refs_0_.3, bf16[128,6144]{1,0:T(8,128)(2,1)} %refs_1_.3, bf16[128,6144]{1,0:T(8,128)(2,1)} %refs_2_.3), custom_call_target="tpu_custom_call" | custom-call | bytes 7864320 | tf_op jit(solution)/shard_map/pack/pallas_call | solution.py:76
  3.8 9.3 %all-to-all-start = ((bf16[16,3,128,256]{3,2,1,0:T(8,128)(2,1)}), bf16[16,3,128,256]{3,2,1,0:T(8,128)(2,1)S(1)}, u32[]{:S(2)}, u32[]{:S(2)}) async-start(bf16[16,3,128,256]{3,2,1,0:T(8,128)(2,1)} %pack.3), calls=%async_computation | async-start | bytes 6291456 | tf_op jit(solution)/shard_map/all_to_all | solution.py:47
  13.9 1.4 copy-done.1
  15.3 1.4 copy-done.2
  16.7 1.4 copy-done.3
  18.2 1.3 pack.2
  20.6 65.1 %all-to-all-done.own = bf16[16,3,128,256]{3,2,1,0:T(8,128)(2,1)S(1)} async-done(((bf16[16,3,128,256]{3,2,1,0:T(8,128)(2,1)}), bf16[16,3,128,256]{3,2,1,0:T(8,128)(2,1)S(1)}, u32[]{:S(2)}, u32[]{:S(2)}) %all-to-all-start) | async-done | bytes 3145760 | tf_op jit(solution)/shard_map/all_to_all | solution.py:47
  85.8 4.4 %all-to-all-start.2 = ((bf16[16,3,128,128]{3,2,1,0:T(8,128)(2,1)}), bf16[16,3,128,128]{3,2,1,0:T(8,128)(2,1)}, u32[]{:S(2)}, u32[]{:S(2)}) async-start(bf16[16,3,128,128]{3,2,1,0:T(8,128)(2,1)} %copy-done), calls=%async_computation.2 | async-start | bytes 3145728 | tf_op jit(solution)/shard_map/all_to_all | solution.py:47
  90.2 1.4 fusion.1
  91.6 6.4 %collective-permute-start.2 = (bf16[8,2,128,256]{3,2,1,0:T(8,128)(2,1)}, bf16[8,2,128,256]{3,2,1,0:T(8,128)(2,1)}, u32[]{:S(2)}, u32[]{:S(2)}) collective-permute-start(bf16[8,2,128,256]{3,2,1,0:T(8,128)(2,1)} %get-tuple-element.11), channel_id=1, source_target_pairs={{0,16},{1,17},{2,18},{3,19},{4,20},{5,21},{6,22},{7,23},{8,24},{9,... | collective-permute-start | bytes 3145736 | tf_op jit(solution)/shard_map/ppermute | solution.py:33
  98.0 1.9 %collective-permute-start.1 = (bf16[8,2,128,256]{3,2,1,0:T(8,128)(2,1)}, bf16[8,2,128,256]{3,2,1,0:T(8,128)(2,1)}, u32[]{:S(2)}, u32[]{:S(2)}) collective-permute-start(bf16[8,2,128,256]{3,2,1,0:T(8,128)(2,1)} %get-tuple-element.12), channel_id=1, source_target_pairs={{16,0},{17,1},{18,2},{19,3},{20,4},{21,5},{22,6},{23,7},{24,8},{25... | collective-permute-start | bytes 3145736 | tf_op jit(solution)/shard_map/ppermute | solution.py:33
  100.1 9.9 %collective-permute-done.2.halo = bf16[8,2,128,256]{3,2,1,0:T(8,128)(2,1)} collective-permute-done((bf16[8,2,128,256]{3,2,1,0:T(8,128)(2,1)}, bf16[8,2,128,256]{3,2,1,0:T(8,128)(2,1)}, u32[]{:S(2)}, u32[]{:S(2)}) %collective-permute-start.2) | collective-permute-done | bytes 1048608 | tf_op jit(solution)/shard_map/ppermute | solution.py:33
  110.0 6.5 %attend.4.refs_0_ = bf16[16,128,256]{2,1,0:T(8,128)(2,1)S(1)} custom-call(s32[192]{0:T(256)S(1)} %reshape.27.list_ref, bf16[16,3,128,256]{3,2,1,0:T(8,128)(2,1)S(1)} %all-to-all-done.own, bf16[8,2,128,256]{3,2,1,0:T(8,128)(2,1)} %collective-permute-done.2.halo), custom_call_target="tpu_custom_call" | custom-call | flops 1610612736 | bytes 4194304 | tf_op jit(solution)/shard_map/attend/pallas_call | solution.py:225
  116.6 1.3 collective-permute-done.1.halo
  117.9 6.5 %attend.5 = bf16[16,128,256]{2,1,0:T(8,128)(2,1)S(1)} custom-call(s32[192]{0:T(256)S(1)} %reshape.26.list_ref, bf16[16,3,128,256]{3,2,1,0:T(8,128)(2,1)S(1)} %all-to-all-done.own, bf16[8,2,128,256]{3,2,1,0:T(8,128)(2,1)} %collective-permute-done.1.halo, bf16[16,128,256]{2,1,0:T(8,128)(2,1)S(1)} %attend.4.refs_0_), custom_call_target="tpu_custom_call", output_to_operand_aliasing={{}: (3, {})} | custom-call | flops 1610612736 | bytes 4194304 | tf_op jit(solution)/shard_map/attend/pallas_call | solution.py:225
  125.6 7.4 %all-to-all-start.1 = ((bf16[16,128,256]{2,1,0:T(8,128)(2,1)}), bf16[16,128,256]{2,1,0:T(8,128)(2,1)S(1)}, u32[]{:S(2)}, u32[]{:S(2)}) async-start(bf16[16,128,256]{2,1,0:T(8,128)(2,1)} %copy-done.4), calls=%async_computation.1 | async-start | bytes 2097152 | tf_op jit(solution)/shard_map/all_to_all | solution.py:47
  133.1 1.3 fusion.2
  134.3 6.9 %collective-permute-start.4 = (bf16[8,2,128,128]{3,2,1,0:T(8,128)(2,1)S(1)}, bf16[8,2,128,128]{3,2,1,0:T(8,128)(2,1)S(1)}, u32[]{:S(2)}, u32[]{:S(2)}) collective-permute-start(bf16[8,2,128,128]{3,2,1,0:T(8,128)(2,1)S(1)} %get-tuple-element.13), channel_id=1, source_target_pairs={{0,16},{1,17},{2,18},{3,19},{4,20},{5,21},{6,22},{7,23},{8,24},{9,... | collective-permute-start | bytes 1572872 | tf_op jit(solution)/shard_map/ppermute | solution.py:33
  141.3 2.1 %collective-permute-start.3 = (bf16[8,2,128,128]{3,2,1,0:T(8,128)(2,1)S(1)}, bf16[8,2,128,128]{3,2,1,0:T(8,128)(2,1)S(1)}, u32[]{:S(2)}, u32[]{:S(2)}) collective-permute-start(bf16[8,2,128,128]{3,2,1,0:T(8,128)(2,1)S(1)} %get-tuple-element.14), channel_id=1, source_target_pairs={{16,0},{17,1},{18,2},{19,3},{20,4},{21,5},{22,6},{23,7},{24,8},{25... | collective-permute-start | bytes 1572872 | tf_op jit(solution)/shard_map/ppermute | solution.py:33
  143.6 3.8 %collective-permute-done.4.halo = bf16[8,2,128,128]{3,2,1,0:T(8,128)(2,1)S(1)} collective-permute-done((bf16[8,2,128,128]{3,2,1,0:T(8,128)(2,1)S(1)}, bf16[8,2,128,128]{3,2,1,0:T(8,128)(2,1)S(1)}, u32[]{:S(2)}, u32[]{:S(2)}) %collective-permute-start.4) | collective-permute-done | bytes 524320 | tf_op jit(solution)/shard_map/ppermute | solution.py:33
  147.4 4.2 %attend.6.refs_0_ = bf16[16,128,128]{2,1,0:T(8,128)(2,1)S(1)} custom-call(s32[96]{0:T(128)S(1)} %reshape.29.list_ref, bf16[16,3,128,128]{3,2,1,0:T(8,128)(2,1)} %all-to-all-done.2.own, bf16[8,2,128,128]{3,2,1,0:T(8,128)(2,1)S(1)} %collective-permute-done.4.halo), custom_call_target="tpu_custom_call" | custom-call | flops 805306368 | bytes 2097152 | tf_op jit(solution)/shard_map/attend/pallas_call | solution.py:225
  151.6 3.5 %collective-permute-done.3.halo = bf16[8,2,128,128]{3,2,1,0:T(8,128)(2,1)S(1)} collective-permute-done((bf16[8,2,128,128]{3,2,1,0:T(8,128)(2,1)S(1)}, bf16[8,2,128,128]{3,2,1,0:T(8,128)(2,1)S(1)}, u32[]{:S(2)}, u32[]{:S(2)}) %collective-permute-start.3) | collective-permute-done | bytes 524320 | tf_op jit(solution)/shard_map/ppermute | solution.py:33
  155.1 4.2 %attend.7 = bf16[16,128,128]{2,1,0:T(8,128)(2,1)S(1)} custom-call(s32[96]{0:T(128)S(1)} %reshape.28.list_ref, bf16[16,3,128,128]{3,2,1,0:T(8,128)(2,1)} %all-to-all-done.2.own, bf16[8,2,128,128]{3,2,1,0:T(8,128)(2,1)S(1)} %collective-permute-done.3.halo, bf16[16,128,128]{2,1,0:T(8,128)(2,1)S(1)} %attend.6.refs_0_), custom_call_target="tpu_custom_call", output_to_operand_aliasing={{}: (3, {})} | custom-call | flops 805306368 | bytes 2097152 | tf_op jit(solution)/shard_map/attend/pallas_call | solution.py:225
  159.3 24.4 %all_to_all.20.refs_1_ = bf16[16,128,128]{2,1,0:T(8,128)(2,1)S(1)} all-to-all(bf16[16,128,128]{2,1,0:T(8,128)(2,1)S(1)} %attend.7), channel_id=1, replica_groups=mesh['blk'=16,'uly'=16] {'uly'}, dimensions={0} | all-to-all | bytes 1048576 | tf_op jit(solution)/shard_map/all_to_all | solution.py:47
  (24 shorter events, 4.7 us)
Async XLA Ops:
  3.8 9.4 %copy-start.5 = (s32[3,16,12]{2,1,0:T(8,128)S(1)}, s32[3,16,12]{2,1,0:T(8,128)}, u32[]{:S(2)}) copy-start(s32[3,16,12]{2,1,0:T(8,128)} %param.8) | copy-start | bytes 6916
  3.8 9.4 %copy-start.6 = (s32[3,16,12]{2,1,0:T(8,128)S(1)}, s32[3,16,12]{2,1,0:T(8,128)}, u32[]{:S(2)}) copy-start(s32[3,16,12]{2,1,0:T(8,128)} %param.9) | copy-start | bytes 6916
  3.8 81.9 %all-to-all-start = ((bf16[16,3,128,256]{3,2,1,0:T(8,128)(2,1)}), bf16[16,3,128,256]{3,2,1,0:T(8,128)(2,1)S(1)}, u32[]{:S(2)}, u32[]{:S(2)}) async-start(bf16[16,3,128,256]{3,2,1,0:T(8,128)(2,1)} %pack.3), calls=%async_computation | async-start | bytes 6291456 | tf_op jit(solution)/shard_map/all_to_all | solution.py:47
  13.3 7.3 %collective-permute-start = (s32[3,16,12]{2,1,0:T(8,128)S(1)}, s32[3,16,12]{2,1,0:T(8,128)S(1)}, u32[]{:S(2)}, u32[]{:S(2)}) collective-permute-start(s32[3,16,12]{2,1,0:T(8,128)S(1)} %clamp_select_fusion), channel_id=1, source_target_pairs={{0,0},{1,1},{2,2},{3,3},{4,4},{5,5},{6,6},{7,7},{8,8},{9,9},{10,10... | collective-permute-start | bytes 6920 | tf_op jit(solution)/shard_map/ppermute | solution.py:43
  13.9 1.4 copy-start.1
  15.3 1.4 copy-start.2
  16.7 1.4 copy-start.3
  19.5 1.1 copy-start
  85.8 39.9 %all-to-all-start.2 = ((bf16[16,3,128,128]{3,2,1,0:T(8,128)(2,1)}), bf16[16,3,128,128]{3,2,1,0:T(8,128)(2,1)}, u32[]{:S(2)}, u32[]{:S(2)}) async-start(bf16[16,3,128,128]{3,2,1,0:T(8,128)(2,1)} %copy-done), calls=%async_computation.2 | async-start | bytes 3145728 | tf_op jit(solution)/shard_map/all_to_all | solution.py:47
  91.6 18.4 %collective-permute-start.2 = (bf16[8,2,128,256]{3,2,1,0:T(8,128)(2,1)}, bf16[8,2,128,256]{3,2,1,0:T(8,128)(2,1)}, u32[]{:S(2)}, u32[]{:S(2)}) collective-permute-start(bf16[8,2,128,256]{3,2,1,0:T(8,128)(2,1)} %get-tuple-element.11), channel_id=1, source_target_pairs={{0,16},{1,17},{2,18},{3,19},{4,20},{5,21},{6,22},{7,23},{8,24},{9,... | collective-permute-start | bytes 3145736 | tf_op jit(solution)/shard_map/ppermute | solution.py:33
  98.0 19.9 %collective-permute-start.1 = (bf16[8,2,128,256]{3,2,1,0:T(8,128)(2,1)}, bf16[8,2,128,256]{3,2,1,0:T(8,128)(2,1)}, u32[]{:S(2)}, u32[]{:S(2)}) collective-permute-start(bf16[8,2,128,256]{3,2,1,0:T(8,128)(2,1)} %get-tuple-element.12), channel_id=1, source_target_pairs={{16,0},{17,1},{18,2},{19,3},{20,4},{21,5},{22,6},{23,7},{24,8},{25... | collective-permute-start | bytes 3145736 | tf_op jit(solution)/shard_map/ppermute | solution.py:33
  124.4 1.0 copy-start.4
  125.6 33.7 %all-to-all-start.1 = ((bf16[16,128,256]{2,1,0:T(8,128)(2,1)}), bf16[16,128,256]{2,1,0:T(8,128)(2,1)S(1)}, u32[]{:S(2)}, u32[]{:S(2)}) async-start(bf16[16,128,256]{2,1,0:T(8,128)(2,1)} %copy-done.4), calls=%async_computation.1 | async-start | bytes 2097152 | tf_op jit(solution)/shard_map/all_to_all | solution.py:47
  134.3 13.0 %collective-permute-start.4 = (bf16[8,2,128,128]{3,2,1,0:T(8,128)(2,1)S(1)}, bf16[8,2,128,128]{3,2,1,0:T(8,128)(2,1)S(1)}, u32[]{:S(2)}, u32[]{:S(2)}) collective-permute-start(bf16[8,2,128,128]{3,2,1,0:T(8,128)(2,1)S(1)} %get-tuple-element.13), channel_id=1, source_target_pairs={{0,16},{1,17},{2,18},{3,19},{4,20},{5,21},{6,22},{7,23},{8,24},{9,... | collective-permute-start | bytes 1572872 | tf_op jit(solution)/shard_map/ppermute | solution.py:33
  141.3 13.8 %collective-permute-start.3 = (bf16[8,2,128,128]{3,2,1,0:T(8,128)(2,1)S(1)}, bf16[8,2,128,128]{3,2,1,0:T(8,128)(2,1)S(1)}, u32[]{:S(2)}, u32[]{:S(2)}) collective-permute-start(bf16[8,2,128,128]{3,2,1,0:T(8,128)(2,1)S(1)} %get-tuple-element.14), channel_id=1, source_target_pairs={{16,0},{17,1},{18,2},{19,3},{20,4},{21,5},{22,6},{23,7},{24,8},{25... | collective-permute-start | bytes 1572872 | tf_op jit(solution)/shard_map/ppermute | solution.py:33
